TPU v7x, 32 devices: a whole 2x2x4 slice. The times are simulated.
32 devices in a mesh: seq: 4 (over x, core), head: 4 (over z), batch: 2 (over y).
Axes of the slice: x: 2, y: 2, z: 4, core: 2. Of those that a mesh axis runs over, the one named last changes fastest.
Arguments:
- hyena_inputs: bfloat16 [4096, 3, 8192], P(('batch', 'seq'), None, 'head'), parts along dimension 0, may hold values from -6 to 6
- short_filter: float32 [3, 3, 8192], P(None, None, 'head'), may hold values from -3.5 to 3.5
- medium_filter: float32 [128, 8192], P(None, 'head'), may hold values from -0.5 to 0.5
- q_proj: bfloat16 [4096, 8192], P(('batch', 'seq'), 'head'), parts along dimension 0, may hold values from -8 to 8
- k_proj: bfloat16 [4096, 8192], P(('batch', 'seq'), 'head'), parts along dimension 0, may hold values from -8 to 8
- out_weight: bfloat16 [8192, 8192], P('head'), may hold values from -0.25 to 0.25
Outputs:
- hyena_out: bfloat16 [4096, 8192], P(('batch', 'seq'), 'head'), parts along dimension 0
- mixed: bfloat16 [4096, 8192], P(('batch', 'seq'), 'head'), parts along dimension 0
There are 2 independent parts, one for each index of `batch`. A program takes and returns all parts, laid end to end along the dimension named above; an argument that names none is the same for every part. Nothing has to cross between parts.
All inputs are finite; a program needn't handle non-finite values.
Results may differ from a plain program's by a relative error of at most 0.011.
Values may be sent and summed in bfloat16 or wider, within the bound.
A program may use at most 192 MiB of HBM per device.

v0:
```python
import math

import jax
import jax.numpy as jnp
from jax import lax
from jax.sharding import PartitionSpec as P

HEAD_SIZE = 128


def passed_along(x, axis, by):
    length = lax.axis_size(axis)
    pairs = [(i, i + by) for i in range(length) if 0 <= i + by < length]
    return lax.ppermute(x, axis, pairs)


def causal_depthwise(extended, taps, out_rows):
    tap_count = taps.shape[0]
    window = extended[extended.shape[0] - out_rows - tap_count + 1 :]
    kernel = taps[::-1][:, None, :]
    result = lax.conv_general_dilated(
        window[None],
        kernel,
        (1,),
        "VALID",
        feature_group_count=extended.shape[1],
        dimension_numbers=("NWC", "WIO", "NWC"),
        precision=lax.Precision.HIGHEST,
    )
    return result[0]


def per_device(hyena_inputs, short_filter, medium_filter, q_proj, k_proj, out_weight):
    tok_rows = hyena_inputs.shape[0]
    chan_width = hyena_inputs.shape[2]
    short_taps = short_filter.shape[1]
    med_taps = medium_filter.shape[0]
    short_table = jnp.transpose(short_filter, (1, 0, 2)).reshape(short_taps, 3 * chan_width)
    input_margin = passed_along(hyena_inputs[tok_rows - (short_taps - 1) :], "seq", 1)
    joined = (
        jnp.concatenate([input_margin, hyena_inputs], 0)
        .astype(jnp.float32)
        .reshape(-1, 3 * chan_width)
    )
    filtered = causal_depthwise(joined, short_table, tok_rows).reshape(tok_rows, 3, chan_width)
    product = (filtered[:, 1] * filtered[:, 2]).astype(jnp.bfloat16)
    product_margin = passed_along(product[tok_rows - (med_taps - 1) :], "seq", 1)
    product_ext = jnp.concatenate([product_margin, product], 0)
    medium = causal_depthwise(product_ext.astype(jnp.float32), medium_filter, tok_rows)
    hyena_out = (filtered[:, 0] * medium).astype(jnp.bfloat16)
    head_count = chan_width // HEAD_SIZE
    score_scale = HEAD_SIZE ** (-0.5)
    seq_index = lax.axis_index("seq")
    queries = q_proj.reshape(tok_rows, head_count, HEAD_SIZE)
    query_pos = seq_index * tok_rows + jnp.arange(tok_rows, dtype=jnp.int32)
    last_query = seq_index * tok_rows + tok_rows - 1
    initial = (
        jnp.zeros((head_count, tok_rows, HEAD_SIZE), jnp.float32),
        jnp.full((head_count, tok_rows), -1e30, jnp.float32),
        jnp.zeros((head_count, tok_rows), jnp.float32),
    )
    carried = initial
    first_row = jnp.int32(0)
    key_piece = lax.all_gather(k_proj, "seq", axis=0, tiled=True)
    value_piece = lax.all_gather(hyena_out, "seq", axis=0, tiled=True)
    piece_rows = key_piece.shape[0]
    block_rows = math.gcd(piece_rows, 512)
    block_count = piece_rows // block_rows
    key_blocks = key_piece.reshape(block_count, block_rows, head_count, HEAD_SIZE)
    value_blocks = value_piece.reshape(block_count, block_rows, head_count, HEAD_SIZE)

    def visit(running, block_item):
        key_blk, value_blk, block_number = block_item
        key_start = first_row + block_number * block_rows

        def attend(current):
            weighted, run_max, total_sum = current
            scores = (
                jnp.einsum("qhd,khd->hqk", queries, key_blk, preferred_element_type=jnp.float32)
                * score_scale
            )
            key_pos = key_start + jnp.arange(block_rows, dtype=jnp.int32)
            allowed = key_pos[None, None, :] <= query_pos[None, :, None]
            masked = jnp.where(allowed, scores, -jnp.inf)
            new_max = jnp.maximum(run_max, jnp.max(masked, axis=-1))
            weights = jnp.exp(masked - new_max[..., None])
            factor = jnp.exp(run_max - new_max)
            new_total = total_sum * factor + jnp.sum(weights, axis=-1)
            new_weighted = weighted * factor[..., None] + jnp.einsum(
                "hqk,khd->hqd",
                weights.astype(jnp.bfloat16),
                value_blk,
                preferred_element_type=jnp.float32,
            )
            return (new_weighted, new_max, new_total)

        def keep_state(current):
            return current

        return (lax.cond(key_start <= last_query, attend, keep_state, running), None)

    carried, unused = lax.scan(
        visit, carried, (key_blocks, value_blocks, jnp.arange(block_count, dtype=jnp.int32))
    )
    weighted, run_max, total_sum = carried
    attended = (
        (weighted / total_sum[..., None])
        .transpose(1, 0, 2)
        .reshape(tok_rows, chan_width)
        .astype(jnp.bfloat16)
    )
    summed = lax.psum_scatter(
        lax.dot_general(
            out_weight, attended, (((0,), (1,)), ((), ())), preferred_element_type=jnp.float32
        ).astype(jnp.bfloat16),
        "head",
        scatter_dimension=0,
        tiled=True,
    ).astype(jnp.float32)
    return (hyena_out, summed.T.astype(jnp.bfloat16))


def solution(mesh):
    return jax.shard_map(
        per_device,
        mesh=mesh,
        in_specs=(
            P(("batch", "seq"), None, "head"),
            P(None, None, "head"),
            P(None, "head"),
            P(("batch", "seq"), "head"),
            P(("batch", "seq"), "head"),
            P("head", None),
        ),
        out_specs=(P(("batch", "seq"), "head"), P(("batch", "seq"), "head")),
        check_vma=False,
    )
```

profile of v0, /device:TPU:14, one launch (start us, length us, event | category | flops | bytes accessed | tf_op | source)
XLA Modules:
  0.0 633.4 jit_solution(6922452532543686896)
XLA Ops:
  7.2 0.0 all-gather.3.cloned.1.call-start
  7.2 0.9 slice.18
  8.1 1.9 collective-permute-start
  10.1 0.0 all-gather.3.cloned.1.call-update
  10.1 0.0 all-gather.5.cloned.1.call-start
  10.1 16.9 %rev.6 = f32[3,6144]{1,0:T(4,128)S(1)} reverse(f32[3,6144]{1,0:T(4,128)} %bitcast.76), dimensions={0} | reverse | bytes 147456 | tf_op jit(solution)/shard_map/rev | solution.py:20
  27.1 0.1 broadcast_in_dim.40
  27.1 7.9 %pad_maximum_fusion = bf16[514,3,2048]{2,0,1:T(8,128)(2,1)} fusion(bf16[512,3,2048]{2,0,1:T(8,128)(2,1)} %param.10, bf16[2,3,2048]{2,0,1:T(2,128)(2,1)S(1)} %collective-permute-done), kind=kLoop, calls=%fused_computation.37 | loop fusion | flops 12632064 | bytes 12632064 | tf_op jit(solution)/shard_map/concatenate | solution.py:41
  35.1 9.7 %copy.12 = bf16[514,3,2048]{0,2,1:T(8,128)(2,1)} copy(bf16[514,3,2048]{2,0,1:T(8,128)(2,1)} %pad_maximum_fusion) | data formatting | bytes 12632064 | tf_op jit(solution)/shard_map/concatenate | solution.py:41
  44.8 7.1 %pad = bf16[1,520,6144]{1,2,0:T(8,128)(2,1)} pad(bf16[1,514,6144]{1,2,0:T(8,128)(2,1)} %bitcast.69, bf16[]{:T(256)} %constant.51), padding=0_0x0_6x0_0 | pad | bytes 12705794 | tf_op jit(solution)/shard_map/broadcast_in_dim;reshape | solution.py:22
  51.9 20.5 %reshape.76 = bf16[1,8,65,6144]{2,1,3,0:T(8,128)(2,1)} reshape(bf16[1,520,6144]{1,2,0:T(8,128)(2,1)} %pad) | data formatting | bytes 12779520 | tf_op jit(solution)/shard_map/conv_general_dilated | solution.py:21
  72.4 16.8 %copy.15 = bf16[1,8,65,6144]{3,1,2,0:T(8,128)(2,1)} copy(bf16[1,8,65,6144]{2,1,3,0:T(8,128)(2,1)} %reshape.76) | data formatting | bytes 12779520 | tf_op jit(solution)/shard_map/conv_general_dilated | solution.py:21
  89.2 1.0 slice.26
  90.2 11.5 %fusion.30 = f32[8,65,6144]{2,0,1:T(8,128)} fusion(f32[3,1,6144]{2,1,0:T(1,128)S(1)} %broadcast_in_dim.40, bf16[1,7,2,6144]{3,1,2,0:T(8,128)(2,1)S(1)} %slice.26, bf16[1,8,65,6144]{3,1,2,0:T(8,128)(2,1)} %copy.15, pred[8,65]{0,1:T(8,128)(4,1)S(1)} %copy-done.4), kind=kOutput, calls=%fused_computation.33 | convolution fusion | flops 137969664 | bytes 19415560 | tf_op jit(solution)/shard_map/conv_general_dilated | solution.py:21
  101.7 17.2 %copy.16 = f32[8,65,6144]{2,1,0:T(8,128)} copy(f32[8,65,6144]{2,0,1:T(8,128)} %fusion.30) | data formatting | bytes 25559040 | tf_op jit(solution)/shard_map/conv_general_dilated | solution.py:21
  118.9 11.3 %reshape.72 = f32[1,520,6144]{2,1,0:T(8,128)} reshape(f32[8,65,6144]{2,1,0:T(8,128)} %copy.16) | data formatting | bytes 25559040 | tf_op jit(solution)/shard_map/conv_general_dilated | solution.py:21
  130.1 10.6 %slice.27 = f32[1,512,6144]{2,1,0:T(8,128)} slice(f32[1,520,6144]{2,1,0:T(8,128)} %reshape.72), slice={[0:1], [0:512], [0:6144]} | slice | bytes 25165824 | tf_op jit(solution)/shard_map/conv_general_dilated | solution.py:21
  140.7 12.8 %copy.17 = f32[1,512,6144]{1,2,0:T(8,128)} copy(f32[1,512,6144]{2,1,0:T(8,128)} %slice.27) | data formatting | bytes 25165824 | tf_op jit(solution)/shard_map/conv_general_dilated | solution.py:21
  153.6 0.0 copy-start.2
  153.6 7.7 %fusion.44 = (f32[512,1,2048]{0,2,1:T(8,128)}, bf16[512,1,2048]{0,2,1:T(8,128)(2,1)S(1)}) fusion(f32[512,3,2048]{0,2,1:T(8,128)} %bitcast.66), kind=kLoop, calls=%fused_computation.51 | loop fusion | flops 2097152 | bytes 18874368 | tf_op jit(solution)/shard_map/slice | solution.py:50
  161.3 1.0 slice_bitcast_fusion
  162.3 1.9 collective-permute-start.1
  164.2 5.2 rev.7
  169.4 5.5 copy.33
  174.9 4.0 maximum_bitcast_fusion
  178.9 11.5 %copy.20 = bf16[1,639,2048]{2,0,1:T(2,128)(2,1)} copy(bf16[1,639,2048]{1,2,0:T(8,128)(2,1)} %maximum_bitcast_fusion) | data formatting | bytes 5234688 | tf_op jit(solution)/shard_map/broadcast_in_dim | solution.py:22
  190.4 48.5 %fusion.39 = f32[1,512,2048]{2,0,1:T(1,128)S(1)} fusion(bf16[1,639,2048]{2,0,1:T(2,128)(2,1)} %copy.20, f32[128,1,2048]{2,0,1:T(8,128)S(1)} %bitcast.75), kind=kOutput, calls=%fused_computation.45 | convolution fusion | flops 1610612736 | bytes 7860224 | tf_op jit(solution)/shard_map/conv_general_dilated | solution.py:21
  238.9 2.7 fusion.37
  241.7 0.0 all-gather.5.cloned.1.call-update
  241.7 0.0 reduce-scatter.2.cloned.1.call-start
  241.8 3.0 copy.22
  244.7 3.0 copy.24
  247.8 0.0 all-gather.3.cloned.1.call-done
  247.8 10.8 %copy.34 = bf16[256,8,16,128]{3,2,1,0:T(8,128)(2,1)} copy(bf16[256,8,16,128]{3,1,2,0:T(8,128)(2,1)} %bitcast.71) | data formatting | bytes 16777216
  258.6 8.8 %copy.23 = bf16[4,512,16,128]{3,1,2,0:T(8,128)(2,1)} copy(bf16[4,512,16,128]{3,2,1,0:T(8,128)(2,1)} %bitcast.67) | data formatting | bytes 16777216
  267.3 34.3 %all-gather.5.cloned.1.call-done = bf16[2048,2048]{1,0:T(8,128)(2,1)} async-done(((bf16[512,2048]{1,0:T(8,128)(2,1)}), bf16[2048,2048]{1,0:T(8,128)(2,1)}) %all-gather.5.cloned.1.call-update) | async-done | bytes 8388624 | tf_op jit(solution)/shard_map/all_gather | solution.py:65
  301.6 9.8 %copy.35 = bf16[256,8,16,128]{3,2,1,0:T(8,128)(2,1)} copy(bf16[256,8,16,128]{3,1,2,0:T(8,128)(2,1)} %bitcast.72) | data formatting | bytes 16777216
  311.4 8.8 %copy.25 = bf16[4,512,16,128]{3,1,2,0:T(8,128)(2,1)} copy(bf16[4,512,16,128]{3,2,1,0:T(8,128)(2,1)} %bitcast.68) | data formatting | bytes 16777216
  320.2 2.5 broadcast_in_dim.43
  322.7 94.8 %while.15 = (s32[]{:T(128)}, f32[16,512,128]{2,1,0:T(8,128)}, f32[16,512]{1,0:T(8,128)S(1)}, f32[16,512]{1,0:T(8,128)S(1)}, s32[4]{0:T(128)S(1)}, /*index=5*/s32...) while((s32[]{:T(128)}, f32[16,512,128]{2,1,0:T(8,128)}, ...), condition=%wide.region_5.6_spmd.clone, body=%wide.region_0.5_spmd.clone.sunk | while | flops 2195997696 | bytes 66598184 | solution.py:102
  322.8 0.6 dynamic_slice.35
  324.1 30.0 %conditional.3 = ((f32[16,512,128]{2,1,0:T(8,128)}, f32[16,512]{1,0:T(8,128)S(1)}, f32[16,512]{1,0:T(8,128)S(1)})) conditional(s32[]{:T(128)} %convert_element_type.60, (f32[16,512,128]{2,1,0:T(8,128)}, f32[16,512]{1,0:T(8,128)S(1)}, f32[16,512]{1,0:T(8,128)S(1)}) %tuple.46, (s32[]{:T(128)}, s32[]{:T(128)}, bf16[4,512,16,128]{3,1,2,0:T(8,128)(2,1)}, ...), branch_computations={%region_1.1_spmd, %region_2.4_spmd} | conditional | flops 2195997696 | bytes 66595880 | solution.py:100
  324.1 0.2 broadcast_compare_fusion
  324.3 8.8 %fusion.4 = (f32[16,512]{1,0:T(8,128)S(1)}, f32[16,512,512]{2,1,0:T(8,128)}) fusion(pred[512,512]{0,1:T(8,128)(4,1)S(1)} %broadcast_compare_fusion, bf16[512,16,128]{2,0,1:T(8,128)(2,1)S(1)} %get-tuple-element.117, bf16[4,512,16,128]{3,1,2,0:T(8,128)(2,1)} %get-tuple-element.115, s32[]{:T(128)} %get-tuple-element.116), kind=kOutput, calls=%fused_computation.5 | convolution fusion | flops 1086316544 | bytes 21266944 | tf_op jit(solution)/shard_map/while/body/eval_jaxpr/cond/branch_1_fun/qhd,khd->hqk/dot_general | solution.py:79
  333.1 9.1 %fusion.2 = f32[16,512]{1,0:T(8,128)S(1)} fusion(f32[16,512,512]{2,1,0:T(8,128)} %get-tuple-element.212, f32[16,512]{1,0:T(8,128)S(1)} %max.4, pred[512,512]{0,1:T(8,128)(4,1)S(1)} %broadcast_compare_fusion), kind=kLoop, calls=%fused_computation.3 | loop fusion | flops 16769024 | bytes 17104896 | tf_op jit(solution)/shard_map/while/body/eval_jaxpr/cond/branch_1_fun/reduce_sum | solution.py:88
  342.3 11.7 %multiply_add_fusion = f32[16,512,128]{2,1,0:T(8,128)} fusion(f32[16,512,128]{2,1,0:T(8,128)} %get-tuple-element.111, f32[16,512]{1,0:T(8,128)S(1)} %get-tuple-element.210, bf16[4,512,16,128]{3,1,2,0:T(8,128)(2,1)} %get-tuple-element.118, s32[]{:T(128)} %get-tuple-element.116, f32[16,512,512]{2,1,0:T(8,128)} %get-tuple-element.212, f32[16,512]{1,0:T(8,128)S(1)} %max.4, ...), kind=kOutput, calls=%fused_computation.11 | convolution fusion | flops 1092616192 | bytes 27591168 | tf_op jit(solution)/shard_map/while/body/eval_jaxpr/cond/branch_1_fun/hqk,khd->hqd/dot_general | solution.py:89
  354.0 0.6 dynamic_slice.35
  355.2 29.9 %conditional.3 = ((f32[16,512,128]{2,1,0:T(8,128)}, f32[16,512]{1,0:T(8,128)S(1)}, f32[16,512]{1,0:T(8,128)S(1)})) conditional(s32[]{:T(128)} %convert_element_type.60, (f32[16,512,128]{2,1,0:T(8,128)}, f32[16,512]{1,0:T(8,128)S(1)}, f32[16,512]{1,0:T(8,128)S(1)}) %tuple.46, (s32[]{:T(128)}, s32[]{:T(128)}, bf16[4,512,16,128]{3,1,2,0:T(8,128)(2,1)}, ...), branch_computations={%region_1.1_spmd, %region_2.4_spmd} | conditional | flops 2195997696 | bytes 66595880 | solution.py:100
  355.3 0.2 broadcast_compare_fusion
  355.5 8.8 %fusion.4 = (f32[16,512]{1,0:T(8,128)S(1)}, f32[16,512,512]{2,1,0:T(8,128)}) fusion(pred[512,512]{0,1:T(8,128)(4,1)S(1)} %broadcast_compare_fusion, bf16[512,16,128]{2,0,1:T(8,128)(2,1)S(1)} %get-tuple-element.117, bf16[4,512,16,128]{3,1,2,0:T(8,128)(2,1)} %get-tuple-element.115, s32[]{:T(128)} %get-tuple-element.116), kind=kOutput, calls=%fused_computation.5 | convolution fusion | flops 1086316544 | bytes 21266944 | tf_op jit(solution)/shard_map/while/body/eval_jaxpr/cond/branch_1_fun/qhd,khd->hqk/dot_general | solution.py:79
  364.3 9.1 %fusion.2 = f32[16,512]{1,0:T(8,128)S(1)} fusion(f32[16,512,512]{2,1,0:T(8,128)} %get-tuple-element.212, f32[16,512]{1,0:T(8,128)S(1)} %max.4, pred[512,512]{0,1:T(8,128)(4,1)S(1)} %broadcast_compare_fusion), kind=kLoop, calls=%fused_computation.3 | loop fusion | flops 16769024 | bytes 17104896 | tf_op jit(solution)/shard_map/while/body/eval_jaxpr/cond/branch_1_fun/reduce_sum | solution.py:88
  373.4 11.7 %multiply_add_fusion = f32[16,512,128]{2,1,0:T(8,128)} fusion(f32[16,512,128]{2,1,0:T(8,128)} %get-tuple-element.111, f32[16,512]{1,0:T(8,128)S(1)} %get-tuple-element.210, bf16[4,512,16,128]{3,1,2,0:T(8,128)(2,1)} %get-tuple-element.118, s32[]{:T(128)} %get-tuple-element.116, f32[16,512,512]{2,1,0:T(8,128)} %get-tuple-element.212, f32[16,512]{1,0:T(8,128)S(1)} %max.4, ...), kind=kOutput, calls=%fused_computation.11 | convolution fusion | flops 1092616192 | bytes 27591168 | tf_op jit(solution)/shard_map/while/body/eval_jaxpr/cond/branch_1_fun/hqk,khd->hqd/dot_general | solution.py:89
  385.1 0.6 dynamic_slice.35
  386.3 29.9 %conditional.3 = ((f32[16,512,128]{2,1,0:T(8,128)}, f32[16,512]{1,0:T(8,128)S(1)}, f32[16,512]{1,0:T(8,128)S(1)})) conditional(s32[]{:T(128)} %convert_element_type.60, (f32[16,512,128]{2,1,0:T(8,128)}, f32[16,512]{1,0:T(8,128)S(1)}, f32[16,512]{1,0:T(8,128)S(1)}) %tuple.46, (s32[]{:T(128)}, s32[]{:T(128)}, bf16[4,512,16,128]{3,1,2,0:T(8,128)(2,1)}, ...), branch_computations={%region_1.1_spmd, %region_2.4_spmd} | conditional | flops 2195997696 | bytes 66595880 | solution.py:100
  386.4 0.2 broadcast_compare_fusion
  386.6 8.8 %fusion.4 = (f32[16,512]{1,0:T(8,128)S(1)}, f32[16,512,512]{2,1,0:T(8,128)}) fusion(pred[512,512]{0,1:T(8,128)(4,1)S(1)} %broadcast_compare_fusion, bf16[512,16,128]{2,0,1:T(8,128)(2,1)S(1)} %get-tuple-element.117, bf16[4,512,16,128]{3,1,2,0:T(8,128)(2,1)} %get-tuple-element.115, s32[]{:T(128)} %get-tuple-element.116), kind=kOutput, calls=%fused_computation.5 | convolution fusion | flops 1086316544 | bytes 21266944 | tf_op jit(solution)/shard_map/while/body/eval_jaxpr/cond/branch_1_fun/qhd,khd->hqk/dot_general | solution.py:79
  395.4 9.1 %fusion.2 = f32[16,512]{1,0:T(8,128)S(1)} fusion(f32[16,512,512]{2,1,0:T(8,128)} %get-tuple-element.212, f32[16,512]{1,0:T(8,128)S(1)} %max.4, pred[512,512]{0,1:T(8,128)(4,1)S(1)} %broadcast_compare_fusion), kind=kLoop, calls=%fused_computation.3 | loop fusion | flops 16769024 | bytes 17104896 | tf_op jit(solution)/shard_map/while/body/eval_jaxpr/cond/branch_1_fun/reduce_sum | solution.py:88
  404.6 11.7 %multiply_add_fusion = f32[16,512,128]{2,1,0:T(8,128)} fusion(f32[16,512,128]{2,1,0:T(8,128)} %get-tuple-element.111, f32[16,512]{1,0:T(8,128)S(1)} %get-tuple-element.210, bf16[4,512,16,128]{3,1,2,0:T(8,128)(2,1)} %get-tuple-element.118, s32[]{:T(128)} %get-tuple-element.116, f32[16,512,512]{2,1,0:T(8,128)} %get-tuple-element.212, f32[16,512]{1,0:T(8,128)S(1)} %max.4, ...), kind=kOutput, calls=%fused_computation.11 | convolution fusion | flops 1092616192 | bytes 27591168 | tf_op jit(solution)/shard_map/while/body/eval_jaxpr/cond/branch_1_fun/hqk,khd->hqd/dot_general | solution.py:89
  416.2 0.6 dynamic_slice.35
  417.5 5.4 copy.26
  422.8 2.8 divide_convert_fusion
  425.7 26.0 %fusion.25 = bf16[8192,512]{0,1:T(8,128)(2,1)} fusion(bf16[512,2048]{0,1:T(8,128)(2,1)S(1)} %bitcast.74, bf16[2048,8192]{1,0:T(8,128)(2,1)} %param.15), kind=kOutput, calls=%fused_computation.29 | convolution fusion | flops 17184063488 | bytes 44040192 | tf_op jit(solution)/shard_map/dot_general | solution.py:113
  451.7 0.0 reduce-scatter.2.cloned.1.call-update
  451.7 175.0 %reduce-scatter.2.cloned.1.call-done = bf16[2048,512]{0,1:T(8,128)(2,1)} async-done(((bf16[8192,512]{0,1:T(8,128)(2,1)}), bf16[2048,512]{0,1:T(8,128)(2,1)}) %reduce-scatter.2.cloned.1.call-update) | async-done | bytes 2097168 | tf_op jit(solution)/shard_map/reduce_scatter | solution.py:112
  (31 shorter events, 0.2 us)
Async XLA Ops:
  7.2 240.6 %all-gather.3.cloned.1.call-start = ((), (), s32[]{:S(2)}) async-start(), calls=%async_computation.1 | async-start | bytes 10485760 | tf_op jit(solution)/shard_map/all_gather | solution.py:64
  8.1 19.0 %collective-permute-start = (bf16[2,3,2048]{2,0,1:T(2,128)(2,1)S(1)}, bf16[2,3,2048]{2,0,1:T(2,128)(2,1)S(1)}, u32[]{:S(2)}, u32[]{:S(2)}) collective-permute-start(bf16[2,3,2048]{2,0,1:T(2,128)(2,1)S(1)} %slice.18), channel_id=1, source_target_pairs={{0,8},{8,16},{16,24},{1,9},{9,17},{17,25},{2,10},{10,18},{18,26},{... | collective-permute-start | bytes 73736 | tf_op jit(solution)/shard_map/ppermute | solution.py:14
  10.1 291.5 %all-gather.5.cloned.1.call-start = ((), (), s32[]{:S(2)}) async-start(), calls=%async_computation.2 | async-start | bytes 10485760 | tf_op jit(solution)/shard_map/all_gather | solution.py:65
  72.4 17.8 %copy-start.4 = (pred[8,65]{0,1:T(8,128)(4,1)S(1)}, pred[8,65]{0,1:T(8,128)(4,1)}, u32[]{:S(2)}) copy-start(pred[8,65]{0,1:T(8,128)(4,1)} %constant.55) | copy-start | bytes 1564
  153.6 10.6 %copy-start.2 = (f32[128,2048]{1,0:T(8,128)S(1)}, f32[128,2048]{1,0:T(8,128)}, u32[]{:S(2)}) copy-start(f32[128,2048]{1,0:T(8,128)} %param.12) | copy-start | bytes 3145732
  162.3 12.6 %collective-permute-start.1 = (bf16[127,2048]{0,1:T(8,128)(2,1)}, bf16[127,2048]{0,1:T(8,128)(2,1)}, u32[]{:S(2)}, u32[]{:S(2)}) collective-permute-start(bf16[127,2048]{0,1:T(8,128)(2,1)} %slice_bitcast_fusion), channel_id=1, source_target_pairs={{0,8},{8,16},{16,24},{1,9},{9,17},{17,25},{2,10},{10,18},{18,26},{... | collective-permute-start | bytes 1560584 | tf_op jit(solution)/shard_map/ppermute | solution.py:14
  174.9 15.6 %copy-start.3 = (f32[128,2048]{1,0:T(8,128)S(1)}, f32[128,2048]{1,0:T(8,128)}, u32[]{:S(2)}) copy-start(f32[128,2048]{1,0:T(8,128)} %rev.7) | copy-start | bytes 3145732
  190.4 48.5 %copy-start = (f32[512,1,2048]{2,0,1:T(8,128)S(1)}, f32[512,1,2048]{2,0,1:T(8,128)}, u32[]{:S(2)}) copy-start(f32[512,1,2048]{2,0,1:T(8,128)} %copy.33) | copy-start | bytes 12582916
  238.9 2.8 copy-start.1
  241.7 385.0 %reduce-scatter.2.cloned.1.call-start = ((), (), s32[]{:S(2)}) async-start(), calls=%async_computation.3 | async-start | bytes 10485760 | tf_op jit(solution)/shard_map/reduce_scatter | solution.py:112
Sparse Core Ops, SparseCore 0:
  10.2 58.7 all-gather.2
  241.8 59.7 all-gather.4
  451.8 174.7 reduce-scatter.1
where the time goes:
time: 644 us; the launch traced here: 633 us
  waiting for transfers between devices  209 us (32%)
  local copies, waits for them, and re-layouts  202 us (31%)
  matrix products  147 us (23%)
  other arithmetic  53.4 us (8%)
  between operations  14.1 us (2%)
    reduce_scatter x1, waiting for transfers between devices, per_device(): lax.psum_scatter(lax.dot_general(out_weight, attended, (((0,), (1,)), (()...  175 us
    conv_general_dilated x7, local copies, waits for them, and re-layouts, causal_depthwise(): lax.conv_general_dilated(window[None], kernel, (1,), 'VALID', feature_gro...  90.2 us
    conv_general_dilated x2, matrix products, causal_depthwise(): lax.conv_general_dilated(window[None], kernel, (1,), 'VALID', feature_gro...  60 us
    unnamed x17, local copies, waits for them, and re-layouts  49.6 us
    dot_general x3, matrix products, attend(): jnp.einsum('hqk,khd->hqd', weights.astype(jnp.bfloat16), value_blk, prefe...  35.1 us
    all_gather x1, waiting for transfers between devices, per_device(): value_piece = lax.all_gather(hyena_out, 'seq', axis=0, tiled=True)  34.3 us
    reduce_sum x3, other arithmetic, attend(): new_total = total_sum * factor + jnp.sum(weights, axis=-1)  27.4 us
    dot_general x3, matrix products, attend(): jnp.einsum('qhd,khd->hqk', queries, key_blk, preferred_element_type=jnp.f...  26.3 us
  transfers between devices with their start and end apart: 5, of which 2 were waited for; matrix products, arithmetic and copies ran while one was open for 40% of the time, Pallas kernels for 0%

commit v1 on v0

v1 whole, which is shorter than its diff:
```python
import functools

import jax
import jax.numpy as jnp
import numpy as np
from jax import lax
from jax.experimental import pallas as pl
from jax.experimental.pallas import tpu as pltpu
from jax.sharding import PartitionSpec as P

HEAD_SIZE = 128
MARGIN = 16
F32 = jnp.float32
BF16 = jnp.bfloat16


def passed_along(x, axis, by):
    length = lax.axis_size(axis)
    pairs = [(i, i + by) for i in range(length) if 0 <= i + by < length]
    return lax.ppermute(x, axis, pairs)


def high_low(x):
    high = x.astype(BF16)
    return high, (x - high.astype(F32)).astype(BF16)


def dot(a, b):
    return jnp.dot(a, b, preferred_element_type=F32)


def transform_tables(taps):
    size = 2 * taps
    freq = (2 * np.arange(taps)[:, None] + 1) * np.pi / size
    rows = np.arange(size)[None, :]
    forward = np.concatenate([np.cos(freq * rows), -np.sin(freq * rows)], 0)
    late = np.arange(taps, size)[:, None]
    inverse = np.concatenate([np.cos(freq.T * late), -np.sin(freq.T * late)], 1) * (2.0 / size)

    def split(table):
        high = table.astype(jnp.bfloat16)
        low = (table - high.astype(np.float64)).astype(jnp.bfloat16)
        return np.stack([high, low])

    return split(forward), split(inverse)


def short_filtered(ext, taps_ref, which):
    total = taps_ref[which, 0:1, :] * ext[MARGIN:]
    for lag in range(1, taps_ref.shape[1]):
        total += taps_ref[which, lag : lag + 1, :] * pltpu.roll(ext, lag, 0)[MARGIN:]
    return total


def tail_kernel(x_ref, short_ref, out_ref):
    parts = [short_filtered(x_ref[i].astype(F32), short_ref, i) for i in (1, 2)]
    out_ref[...] = (parts[0] * parts[1]).astype(BF16)


def filter_kernel(x_ref, halo_ref, tail_ref, short_ref, medium_ref, fwd_ref, inv_ref, out_ref):
    taps = medium_ref.shape[0]
    rows = x_ref.shape[1]
    filtered = []
    for i in range(3):
        ext = jnp.concatenate([halo_ref[i].astype(F32), x_ref[i].astype(F32)], 0)
        filtered.append(short_filtered(ext, short_ref, i))
    product = (filtered[1] * filtered[2]).astype(BF16)
    med_high, med_low = high_low(medium_ref[...])
    fwd_high, fwd_low = fwd_ref[0], fwd_ref[1]
    spectrum = (
        dot(fwd_high[:, :taps], med_high)
        + dot(fwd_high[:, :taps], med_low)
        + dot(fwd_low[:, :taps], med_high)
    )
    h_re, h_im = spectrum[:taps], spectrum[taps:]
    for b in range(rows // taps):
        before = tail_ref[...] if b == 0 else product[(b - 1) * taps : b * taps]
        window = jnp.concatenate([before, product[b * taps : (b + 1) * taps]], 0)
        x = dot(fwd_high, window) + dot(fwd_low, window)
        x_re, x_im = x[:taps], x[taps:]
        y = jnp.concatenate([x_re * h_re - x_im * h_im, x_re * h_im + x_im * h_re], 0)
        y_high, y_low = high_low(y)
        medium = dot(inv_ref[0], y_high) + dot(inv_ref[0], y_low) + dot(inv_ref[1], y_high)
        span = slice(b * taps, (b + 1) * taps)
        out_ref[span, :] = (filtered[0][span] * medium).astype(BF16)


def filter_block(hyena_inputs, short_filter, medium_filter):
    x = jnp.transpose(hyena_inputs, (1, 0, 2))
    _, rows, width = x.shape
    taps = medium_filter.shape[0]
    tile = min(256, width)
    halo = passed_along(x[:, rows - MARGIN :], "seq", 1)
    tail_rows = x[:, rows - taps - MARGIN :]
    by_col = lambda *lead: pl.BlockSpec((*lead, tile), lambda c: (0,) * len(lead) + (c,))
    whole = lambda a: pl.BlockSpec(a.shape, lambda c: (0,) * a.ndim)
    tail = pl.pallas_call(
        tail_kernel,
        grid=(width // tile,),
        out_shape=jax.ShapeDtypeStruct((taps, width), BF16),
        in_specs=[by_col(3, taps + MARGIN), by_col(3, short_filter.shape[1])],
        out_specs=by_col(taps),
    )(tail_rows, short_filter)
    tail = passed_along(tail, "seq", 1)
    forward, inverse = transform_tables(taps)
    return pl.pallas_call(
        filter_kernel,
        grid=(width // tile,),
        out_shape=jax.ShapeDtypeStruct((rows, width), BF16),
        in_specs=[
            by_col(3, rows),
            by_col(3, MARGIN),
            by_col(taps),
            by_col(3, short_filter.shape[1]),
            by_col(taps),
            whole(forward),
            whole(inverse),
        ],
        out_specs=by_col(rows),
        compiler_params=pltpu.CompilerParams(vmem_limit_bytes=56 * 2**20),
    )(x, halo, tail, short_filter, medium_filter, jnp.asarray(forward), jnp.asarray(inverse))


def attention_kernel(block, q_ref, k_ref, v_ref, out_ref, acc, top, total):
    rows = q_ref.shape[0]
    me = lax.axis_index("seq")
    scale = HEAD_SIZE ** (-0.5) * float(np.log2(np.e))
    acc[...] = jnp.zeros_like(acc)
    total[...] = jnp.zeros_like(total)
    top[...] = jnp.full_like(top, -1e30)

    def visit(start, diagonal):
        keys = k_ref[pl.ds(start, block), :]
        s = lax.dot_general(keys, q_ref[...], (((1,), (1,)), ((), ())), preferred_element_type=F32)
        if diagonal is not None:
            key_pos = lax.broadcasted_iota(jnp.int32, s.shape, 0) + diagonal
            query_pos = lax.broadcasted_iota(jnp.int32, s.shape, 1)
            s = jnp.where(key_pos <= query_pos, s, -1e30)
        new_top = jnp.maximum(top[...], jnp.max(s, axis=0, keepdims=True))
        weights = jnp.exp2(s * scale - new_top * scale)
        factor = jnp.exp2((top[...] - new_top) * scale)
        total[...] = total[...] * factor + jnp.sum(weights, axis=0, keepdims=True)
        acc[...] = acc[...] * factor + lax.dot_general(
            v_ref[pl.ds(start, block), :],
            weights.astype(BF16),
            (((0,), (0,)), ((), ())),
            preferred_element_type=F32,
        )
        top[...] = new_top

    def full(i, carry):
        visit(pl.multiple_of(i * block, block), None)
        return carry

    lax.fori_loop(0, me * (rows // block), full, 0)
    for j in range(rows // block):
        visit(pl.multiple_of(me * rows + j * block, block), j * block)
    out_ref[...] = (acc[...] / total[...]).T.astype(BF16)


def attention(q, keys, values):
    rows, width = q.shape
    one = lambda n: pl.BlockSpec((n, HEAD_SIZE), lambda h: (0, h))
    return pl.pallas_call(
        functools.partial(attention_kernel, rows),
        grid=(width // HEAD_SIZE,),
        out_shape=jax.ShapeDtypeStruct((rows, width), BF16),
        in_specs=[one(rows), one(keys.shape[0]), one(keys.shape[0])],
        out_specs=one(rows),
        scratch_shapes=[
            pltpu.VMEM((HEAD_SIZE, rows), F32),
            pltpu.VMEM((1, rows), F32),
            pltpu.VMEM((1, rows), F32),
        ],
        compiler_params=pltpu.CompilerParams(vmem_limit_bytes=56 * 2**20),
    )(q, keys, values)


def per_device(hyena_inputs, short_filter, medium_filter, q_proj, k_proj, out_weight):
    keys = lax.all_gather(k_proj, "seq", axis=0, tiled=True)
    hyena_out = filter_block(hyena_inputs, short_filter, medium_filter)
    values = lax.all_gather(hyena_out, "seq", axis=0, tiled=True)
    attended = attention(q_proj, keys, values)
    summed = lax.psum_scatter(
        lax.dot_general(
            out_weight, attended, (((0,), (1,)), ((), ())), preferred_element_type=F32
        ).astype(BF16),
        "head",
        scatter_dimension=0,
        tiled=True,
    )
    return (hyena_out, summed.T)


def solution(mesh):
    return jax.shard_map(
        per_device,
        mesh=mesh,
        in_specs=(
            P(("batch", "seq"), None, "head"),
            P(None, None, "head"),
            P(None, "head"),
            P(("batch", "seq"), "head"),
            P(("batch", "seq"), "head"),
            P("head", None),
        ),
        out_specs=(P(("batch", "seq"), "head"), P(("batch", "seq"), "head")),
        check_vma=False,
    )
```

time: 644 us -> 364 us (0.57); the launches traced: 633 us -> 361 us
  local copies, waits for them, and re-layouts: 202 us -> 5.37 us
  matrix products: 147 us -> 26 us
  Pallas kernels: 0 us -> 55.9 us
  other arithmetic: 53.4 us -> 0 us
  waiting for transfers between devices: 209 us -> 256 us
    conv_general_dilated x7 -> x0, local copies, waits for them, and re-layouts: 90.2 us -> none  [causal_depthwise(): lax.conv_general_dilated(window[None], kernel, (1,), 'VALID', feature_gro...]
    dot_general x6 -> x0, matrix products: 61.4 us -> none  [the longest x3 35.1 us: attend(): jnp.einsum('hqk,khd->hqd', weights.astype(jnp.bfloat16), value_blk, prefe...]
    conv_general_dilated x2 -> x0, matrix products: 60 us -> none  [causal_depthwise(): lax.conv_general_dilated(window[None], kernel, (1,), 'VALID', feature_gro...]
    pallas_call x0 -> x3, Pallas kernels: none -> 55.9 us  [the longest x1 36.3 us: attention(): pl.pallas_call(functools.partial(attention_kernel, rows), grid=(width //...]
    unnamed x17 -> x4, local copies, waits for them, and re-layouts: 49.6 us -> 1.49 us
    all_gather x2, waiting for transfers between devices: 34.3 us -> 76.2 us  [the longest x1 60.5 us: per_device(): values = lax.all_gather(hyena_out, 'seq', axis=0, tiled=True)]
    reduce_sum x3 -> x0, other arithmetic: 27.4 us -> none  [attend(): new_total = total_sum * factor + jnp.sum(weights, axis=-1)]
    ppermute x2, waiting for transfers between devices: 0.01 us -> 23.3 us  [passed_along(): return lax.ppermute(x, axis, pairs)]
  transfers between devices with their start and end apart: 5 -> 5, of which waited for: 2 -> 4; matrix products, arithmetic and copies ran while one was open for 40% -> 1% of each run, Pallas kernels for 0% -> 5%
where the time goes in v1:
time: 364 us; the launch traced here: 361 us
  waiting for transfers between devices  256 us (70%)
  Pallas kernels  55.9 us (15%)
  matrix products  26 us (7%)
  between operations  13.8 us (4%)
  local copies, waits for them, and re-layouts  5.37 us (1%)
  starting transfers between devices  3.95 us (1%)
    reduce_scatter x1, waiting for transfers between devices, per_device(): lax.psum_scatter(lax.dot_general(out_weight, attended, (((0,), (1,)), (()...  156 us
    all_gather x1, waiting for transfers between devices, per_device(): values = lax.all_gather(hyena_out, 'seq', axis=0, tiled=True)  60.5 us
    pallas_call x1, Pallas kernels, attention(): pl.pallas_call(functools.partial(attention_kernel, rows), grid=(width //...  36.3 us
    dot_general x1, matrix products, per_device(): lax.dot_general(out_weight, attended, (((0,), (1,)), ((), ())), preferred...  26 us
    ppermute x2, waiting for transfers between devices, passed_along(): return lax.ppermute(x, axis, pairs)  23.3 us
    all_gather x1, waiting for transfers between devices, per_device(): keys = lax.all_gather(k_proj, 'seq', axis=0, tiled=True)  15.7 us
    pallas_call x1, Pallas kernels, filter_block(): pl.pallas_call(filter_kernel, grid=(width // tile,), out_shape=jax.ShapeD...  14 us
  transfers between devices with their start and end apart: 5, of which 4 were waited for; matrix products, arithmetic and copies ran while one was open for 1% of the time, Pallas kernels for 5%

profile of v1, /device:TPU:14, one launch (start us, length us, event | category | flops | bytes accessed | tf_op | source)
XLA Modules:
  0.0 361.3 jit_solution(8821558635339848938)
XLA Ops:
  7.2 0.0 all-gather.3.cloned.1.call-start
  7.2 0.7 all-gather.3.cloned.1.call-update
  7.9 0.0 all-gather.5.cloned.1.call-start
  7.9 2.9 slice.9.x_ref
  10.8 5.5 %shard_map.95 = bf16[128,2048]{1,0:T(8,128)(2,1)} custom-call(bf16[3,144,2048]{2,1,0:T(8,128)(2,1)} %slice.9.x_ref, f32[3,3,2048]{2,1,0:T(4,128)} %short_ref.3), custom_call_target="tpu_custom_call" | custom-call | tf_op jit(solution)/shard_map/pallas_call | solution.py:97
  16.4 1.9 collective-permute-start.1
  18.3 1.0 slice.8
  19.3 1.9 collective-permute-start
  21.2 23.3 %collective-permute-done.halo_ref = bf16[3,16,2048]{2,1,0:T(8,128)(2,1)S(1)} collective-permute-done((bf16[3,16,2048]{2,1,0:T(8,128)(2,1)S(1)}, bf16[3,16,2048]{2,1,0:T(8,128)(2,1)S(1)}, u32[]{:S(2)}, u32[]{:S(2)}) %collective-permute-start) | collective-permute-done | bytes 196640 | tf_op jit(solution)/shard_map/ppermute | solution.py:20
  44.5 0.0 copy-start.1
  44.5 0.0 collective-permute-done.1.tail_ref
  44.5 0.7 copy-done.1
  45.2 0.0 copy-start
  45.2 0.8 copy-done
  46.0 14.0 %shard_map.96 = bf16[512,2048]{1,0:T(8,128)(2,1)} custom-call(bf16[3,512,2048]{2,1,0:T(8,128)(2,1)} %bitcast.8, bf16[3,16,2048]{2,1,0:T(8,128)(2,1)} %copy-done.1, bf16[128,2048]{1,0:T(8,128)(2,1)} %copy-done, f32[3,3,2048]{2,1,0:T(4,128)} %short_ref.3, f32[128,2048]{1,0:T(8,128)} %medium_ref.1, bf16[2,256,256]{2,1,0:T(8,128)(2,1)} %constant.4.clone.fwd_ref, ...), custom_call_target="tpu_custom_call" | custom-call | tf_op jit(solution)/shard_map/pallas_call | solution.py:106
  60.0 0.0 all-gather.5.cloned.1.call-update
  60.0 0.0 reduce-scatter.2.cloned.1.call-start
  60.1 15.7 %all-gather.3.cloned.1.call-done.k_ref = bf16[2048,2048]{1,0:T(8,128)(2,1)} async-done(((bf16[512,2048]{1,0:T(8,128)(2,1)}), bf16[2048,2048]{1,0:T(8,128)(2,1)}) %all-gather.3.cloned.1.call-update) | async-done | bytes 8388624 | tf_op jit(solution)/shard_map/all_gather | solution.py:180
  75.8 60.5 %all-gather.5.cloned.1.call-done.v_ref = bf16[2048,2048]{1,0:T(8,128)(2,1)} async-done(((bf16[512,2048]{1,0:T(8,128)(2,1)}), bf16[2048,2048]{1,0:T(8,128)(2,1)}) %all-gather.5.cloned.1.call-update) | async-done | bytes 8388624 | tf_op jit(solution)/shard_map/all_gather | solution.py:182
  136.2 36.3 %shard_map.97 = bf16[512,2048]{1,0:T(8,128)(2,1)} custom-call(bf16[512,2048]{1,0:T(8,128)(2,1)} %q_ref.1, bf16[2048,2048]{1,0:T(8,128)(2,1)} %all-gather.3.cloned.1.call-done.k_ref, bf16[2048,2048]{1,0:T(8,128)(2,1)} %all-gather.5.cloned.1.call-done.v_ref), custom_call_target="tpu_custom_call" | custom-call | tf_op jit(solution)/shard_map/pallas_call | solution.py:164
  172.6 26.0 %fusion = bf16[8192,512]{0,1:T(8,128)(2,1)} fusion(bf16[512,2048]{1,0:T(8,128)(2,1)} %shard_map.97, bf16[2048,8192]{1,0:T(8,128)(2,1)} %param.13), kind=kOutput, calls=%fused_computation.1 | convolution fusion | flops 17184063488 | bytes 44040192 | tf_op jit(solution)/shard_map/dot_general | solution.py:185
  198.6 0.0 reduce-scatter.2.cloned.1.call-update
  198.6 156.2 %reduce-scatter.2.cloned.1.call-done = bf16[2048,512]{0,1:T(8,128)(2,1)} async-done(((bf16[8192,512]{0,1:T(8,128)(2,1)}), bf16[2048,512]{0,1:T(8,128)(2,1)}) %reduce-scatter.2.cloned.1.call-update) | async-done | bytes 2097168 | tf_op jit(solution)/shard_map/reduce_scatter | solution.py:184
Async XLA Ops:
  7.2 68.6 %all-gather.3.cloned.1.call-start = ((), (), s32[]{:S(2)}) async-start(), calls=%async_computation.1 | async-start | bytes 10485760 | tf_op jit(solution)/shard_map/all_gather | solution.py:180
  7.9 128.3 %all-gather.5.cloned.1.call-start = ((), (), s32[]{:S(2)}) async-start(), calls=%async_computation.2 | async-start | bytes 10485760 | tf_op jit(solution)/shard_map/all_gather | solution.py:182
  16.4 28.1 %collective-permute-start.1 = (bf16[128,2048]{1,0:T(8,128)(2,1)}, bf16[128,2048]{1,0:T(8,128)(2,1)S(1)}, u32[]{:S(2)}, u32[]{:S(2)}) collective-permute-start(bf16[128,2048]{1,0:T(8,128)(2,1)} %shard_map.95), channel_id=1, source_target_pairs={{0,8},{8,16},{16,24},{1,9},{9,17},{17,25},{2,10},{10,18},{18,26},{... | collective-permute-start | bytes 1572872 | tf_op jit(solution)/shard_map/ppermute | solution.py:20
  19.3 25.2 %collective-permute-start = (bf16[3,16,2048]{2,1,0:T(8,128)(2,1)S(1)}, bf16[3,16,2048]{2,1,0:T(8,128)(2,1)S(1)}, u32[]{:S(2)}, u32[]{:S(2)}) collective-permute-start(bf16[3,16,2048]{2,1,0:T(8,128)(2,1)S(1)} %slice.8), channel_id=1, source_target_pairs={{0,8},{8,16},{16,24},{1,9},{9,17},{17,25},{2,10},{10,18},{18,26},{... | collective-permute-start | bytes 589832 | tf_op jit(solution)/shard_map/ppermute | solution.py:20
  44.5 0.7 copy-start.1
  45.2 0.8 copy-start
  60.0 294.8 %reduce-scatter.2.cloned.1.call-start = ((), (), s32[]{:S(2)}) async-start(), calls=%async_computation.3 | async-start | bytes 10485760 | tf_op jit(solution)/shard_map/reduce_scatter | solution.py:184
Sparse Core Ops, SparseCore 0:
  9.6 66.1 all-gather.2
  77.9 58.2 all-gather.4
  198.8 155.9 reduce-scatter.1

commit v2 on v1

--- a/solution.py
+++ b/solution.py
@@ -1,4 +1,5 @@
 import functools
+import math
 
 import jax
 import jax.numpy as jnp
@@ -12,6 +13,7 @@
 MARGIN = 16
 F32 = jnp.float32
 BF16 = jnp.bfloat16
+MESH = pl.DeviceIdType.MESH
 
 
 def passed_along(x, axis, by):
@@ -121,75 +123,304 @@
     )(x, halo, tail, short_filter, medium_filter, jnp.asarray(forward), jnp.asarray(inverse))
 
 
-def attention_kernel(block, q_ref, k_ref, v_ref, out_ref, acc, top, total):
+def attention_kernel(chips, groups, q_ref, *refs):
+    pieces = 2 * chips
+    key_refs, own_ref = refs[:pieces], refs[pieces]
+    out_ref, got, acc, top, total, send_sem, recv_sem = refs[pieces + 1 :]
     rows = q_ref.shape[0]
+    group_width = q_ref.shape[1] // groups
     me = lax.axis_index("seq")
+    chip, core = lax.div(me, 2), lax.rem(me, 2)
+    partner = me + 1 - 2 * core
     scale = HEAD_SIZE ** (-0.5) * float(np.log2(np.e))
-    acc[...] = jnp.zeros_like(acc)
-    total[...] = jnp.zeros_like(total)
-    top[...] = jnp.full_like(top, -1e30)
-
-    def visit(start, diagonal):
-        keys = k_ref[pl.ds(start, block), :]
-        s = lax.dot_general(keys, q_ref[...], (((1,), (1,)), ((), ())), preferred_element_type=F32)
-        if diagonal is not None:
-            key_pos = lax.broadcasted_iota(jnp.int32, s.shape, 0) + diagonal
+
+    barrier = pltpu.get_barrier_semaphore()
+    for step in range(1, chips):
+        other = lax.rem(chip + step, chips) * 2 + core
+        pl.semaphore_signal(barrier, inc=1, device_id={"seq": other}, device_id_type=MESH)
+    pl.semaphore_signal(barrier, inc=1, device_id={"seq": partner}, device_id_type=MESH)
+    pl.semaphore_wait(barrier, chips)
+
+    def across(d, g):
+        span = pl.ds(pl.multiple_of(g * group_width, HEAD_SIZE), group_width)
+        return pltpu.make_async_remote_copy(
+            src_ref=own_ref.at[:, span],
+            dst_ref=got.at[d - 1, :, span],
+            send_sem=send_sem.at[d - 1, g],
+            recv_sem=recv_sem.at[d - 1, g],
+            device_id={"seq": lax.rem(chip + d, chips) * 2 + core},
+            device_id_type=MESH,
+        )
+
+    def beside(d, g):
+        span = pl.ds(pl.multiple_of(g * group_width, HEAD_SIZE), group_width)
+        source = own_ref.at[:, span] if d == 0 else got.at[d - 1, :, span]
+        return pltpu.make_async_remote_copy(
+            src_ref=source,
+            dst_ref=got.at[chips - 1 + d, :, span],
+            send_sem=send_sem.at[chips - 1 + d, g],
+            recv_sem=recv_sem.at[chips - 1 + d, g],
+            device_id={"seq": partner},
+            device_id_type=MESH,
+        )
+
+    def send_group(g, carry):
+        for d in range(1, chips):
+            pl.when(chip + d < chips)(lambda d=d: across(d, g).start())
+        pl.when(core == 0)(lambda: beside(0, g).start())
+        return carry
+
+    lax.fori_loop(0, groups, send_group, 0)
+
+    def visit(keys, values, diagonal):
+        s = lax.dot_general(keys[0], keys[1], (((1,), (1,)), ((), ())), preferred_element_type=F32)
+        if diagonal:
+            key_pos = lax.broadcasted_iota(jnp.int32, s.shape, 0)
             query_pos = lax.broadcasted_iota(jnp.int32, s.shape, 1)
             s = jnp.where(key_pos <= query_pos, s, -1e30)
-        new_top = jnp.maximum(top[...], jnp.max(s, axis=0, keepdims=True))
+        new_top = jnp.max(s, axis=0, keepdims=True)
+        if not diagonal:
+            new_top = jnp.maximum(top[...], new_top)
         weights = jnp.exp2(s * scale - new_top * scale)
-        factor = jnp.exp2((top[...] - new_top) * scale)
-        total[...] = total[...] * factor + jnp.sum(weights, axis=0, keepdims=True)
-        acc[...] = acc[...] * factor + lax.dot_general(
-            v_ref[pl.ds(start, block), :],
-            weights.astype(BF16),
-            (((0,), (0,)), ((), ())),
-            preferred_element_type=F32,
+        added = jnp.sum(weights, axis=0, keepdims=True)
+        product = lax.dot_general(
+            values, weights.astype(BF16), (((0,), (0,)), ((), ())), preferred_element_type=F32
         )
+        if diagonal:
+            total[...] = added
+            acc[...] = product
+        else:
+            factor = jnp.exp2((top[...] - new_top) * scale)
+            total[...] = total[...] * factor + added
+            acc[...] = acc[...] * factor + product
         top[...] = new_top
 
-    def full(i, carry):
-        visit(pl.multiple_of(i * block, block), None)
+    def one_group(g, carry):
+        for d in range(1, chips):
+
+            @pl.when(chip >= d)
+            def _():
+                across(d, g).wait_recv()
+                beside(d, g).start()
+
+        pl.when(core == 1)(lambda: beside(0, g).wait_recv())
+        for d in range(1, chips):
+            pl.when(chip >= d)(lambda d=d: beside(d, g).wait_recv())
+
+        def one_head(h, carry):
+            cols = pl.ds(pl.multiple_of(g * group_width + h * HEAD_SIZE, HEAD_SIZE), HEAD_SIZE)
+            queries = q_ref[:, cols]
+            visit((key_refs[0][:, cols], queries), own_ref[:, cols], True)
+
+            @pl.when(core == 1)
+            def _():
+                visit((key_refs[chips][:, cols], queries), got[chips - 1, :, cols], False)
+
+            for d in range(1, chips):
+
+                @pl.when(chip >= d)
+                def _():
+                    visit((key_refs[d][:, cols], queries), got[d - 1, :, cols], False)
+                    visit((key_refs[chips + d][:, cols], queries), got[chips - 1 + d, :, cols], False)
+
+            out_ref[:, cols] = (acc[...] / total[...]).T.astype(BF16)
+            return carry
+
+        return lax.fori_loop(0, group_width // HEAD_SIZE, one_head, carry)
+
+    lax.fori_loop(0, groups, one_group, 0)
+
+    def finish(g, carry):
+        for d in range(1, chips):
+            pl.when(chip + d < chips)(lambda d=d: across(d, g).wait_send())
+            pl.when(chip >= d)(lambda d=d: beside(d, g).wait_send())
+        pl.when(core == 0)(lambda: beside(0, g).wait_send())
         return carry
 
-    lax.fori_loop(0, me * (rows // block), full, 0)
-    for j in range(rows // block):
-        visit(pl.multiple_of(me * rows + j * block, block), j * block)
-    out_ref[...] = (acc[...] / total[...]).T.astype(BF16)
-
-
-def attention(q, keys, values):
+    lax.fori_loop(0, groups, finish, 0)
+
+
+def earlier_pieces(x):
+    chips = lax.axis_size("seq") // 2
+    mine, other = [x], []
+    for d in range(1, chips):
+        pairs = [(2 * i + k, 2 * (i + d) + k) for i in range(chips - d) for k in range(2)]
+        mine.append(lax.ppermute(x, "seq", pairs))
+    for d in range(chips):
+        pairs = [(2 * i, 2 * i + 1) for i in range(d, chips)]
+        if d > 0:
+            pairs += [(2 * i + 1, 2 * i) for i in range(d, chips)]
+        other.append(lax.ppermute(mine[d], "seq", pairs))
+    return mine + other
+
+
+def attention(q, key_pieces, values):
     rows, width = q.shape
-    one = lambda n: pl.BlockSpec((n, HEAD_SIZE), lambda h: (0, h))
+    chips = len(key_pieces) // 2
+    groups = math.gcd(width // HEAD_SIZE, 8)
+    in_vmem = pl.BlockSpec(memory_space=pltpu.VMEM)
     return pl.pallas_call(
-        functools.partial(attention_kernel, rows),
-        grid=(width // HEAD_SIZE,),
+        functools.partial(attention_kernel, chips, groups),
         out_shape=jax.ShapeDtypeStruct((rows, width), BF16),
-        in_specs=[one(rows), one(keys.shape[0]), one(keys.shape[0])],
-        out_specs=one(rows),
+        in_specs=[in_vmem] * (2 * chips + 2),
+        out_specs=in_vmem,
         scratch_shapes=[
+            pltpu.VMEM((2 * chips - 1, rows, width), BF16),
             pltpu.VMEM((HEAD_SIZE, rows), F32),
             pltpu.VMEM((1, rows), F32),
             pltpu.VMEM((1, rows), F32),
+            pltpu.SemaphoreType.DMA((2 * chips - 1, groups)),
+            pltpu.SemaphoreType.DMA((2 * chips - 1, groups)),
         ],
-        compiler_params=pltpu.CompilerParams(vmem_limit_bytes=56 * 2**20),
-    )(q, keys, values)
+        compiler_params=pltpu.CompilerParams(
+            collective_id=1, has_side_effects=True, vmem_limit_bytes=56 * 2**20
+        ),
+    )(q, *key_pieces, values)
+
+
+def project_kernel(n, chunk, att_ref, w_ref, out_ref, w_buf, slots, part, w_sem, send_sem, recv_sem):
+    per_owner = out_ref.shape[1] // chunk
+    me = lax.axis_index("head")
+    up, down = n - 1 - me, me
+    both = jnp.minimum(up, down)
+    steps = n * per_owner
+
+    def order(u):
+        pair = lax.div(u, 2 * per_owner)
+        within = lax.rem(u, 2 * per_owner)
+        paired_owner = jnp.where(lax.rem(within, 2) == 0, n - 1 - pair, pair)
+        single = both + lax.div(jnp.maximum(u - 2 * both * per_owner, 0), per_owner)
+        single_owner = jnp.where(up > down, n - 1 - single, single)
+        in_pairs = u < 2 * both * per_owner
+        owner = jnp.where(in_pairs, paired_owner, single_owner)
+        piece = jnp.where(in_pairs, lax.div(within, 2), lax.rem(u, per_owner))
+        return jnp.where(u >= steps - per_owner, me, owner), piece
+
+    def load(u):
+        owner, piece = order(u)
+        panel = owner * per_owner + piece
+        columns = pl.ds(pl.multiple_of(panel * chunk, 128), chunk)
+        return pltpu.make_async_copy(w_ref.at[:, columns], w_buf.at[panel], w_sem.at[panel]), panel
+
+    def start_load(u, carry):
+        load(u)[0].start()
+        return carry
+
+    lax.fori_loop(0, steps, start_load, 0)
+
+    barrier = pltpu.get_barrier_semaphore()
+
+    @pl.when(me > 0)
+    def _():
+        pl.semaphore_signal(barrier, inc=1, device_id={"head": me - 1}, device_id_type=MESH)
+
+    @pl.when(me < n - 1)
+    def _():
+        pl.semaphore_signal(barrier, inc=1, device_id={"head": me + 1}, device_id_type=MESH)
+
+    ends = (me == 0).astype(jnp.int32) + (me == n - 1).astype(jnp.int32)
+    pl.semaphore_wait(barrier, 2 - ends)
+
+    def passed(owner, piece):
+        target = jnp.where(owner > me, me + 1, me - 1)
+        slot = jnp.where(owner == me - 1, n, owner)
+        return pltpu.make_async_remote_copy(
+            src_ref=slots.at[owner, piece],
+            dst_ref=slots.at[slot, piece],
+            send_sem=send_sem.at[owner, piece],
+            recv_sem=recv_sem.at[slot, piece],
+            device_id={"head": target},
+            device_id_type=MESH,
+        )
+
+    def arrived(slot, piece, source):
+        return pltpu.make_async_remote_copy(
+            src_ref=slots.at[slot, piece],
+            dst_ref=slots.at[slot, piece],
+            send_sem=send_sem.at[slot, piece],
+            recv_sem=recv_sem.at[slot, piece],
+            device_id={"head": source},
+            device_id_type=MESH,
+        )
+
+    def one_step(u, carry):
+        owner, piece = order(u)
+        copy, panel = load(u)
+        copy.wait()
+        part[...] = dot(att_ref[...], w_buf[panel])
+
+        @pl.when(u < steps - per_owner)
+        def _():
+            first = jnp.where(owner > me, me == 0, me == n - 1)
+
+            @pl.when(first)
+            def _():
+                slots[owner, piece] = part[...].astype(BF16)
+
+            @pl.when(jnp.logical_not(first))
+            def _():
+                arrived(owner, piece, jnp.where(owner > me, me - 1, me + 1)).wait_recv()
+                slots[owner, piece] = (part[...] + slots[owner, piece].astype(F32)).astype(BF16)
+
+            passed(owner, piece).start()
+
+        @pl.when(u >= steps - per_owner)
+        def _():
+            @pl.when(me > 0)
+            def _():
+                arrived(me, piece, me - 1).wait_recv()
+                part[...] += slots[me, piece].astype(F32)
+
+            @pl.when(me < n - 1)
+            def _():
+                arrived(n, piece, me + 1).wait_recv()
+                part[...] += slots[n, piece].astype(F32)
+
+            columns = pl.ds(pl.multiple_of(piece * chunk, 128), chunk)
+            out_ref[:, columns] = part[...].astype(BF16)
+
+        return carry
+
+    lax.fori_loop(0, steps, one_step, 0)
+
+    def finish(u, carry):
+        passed(*order(u)).wait_send()
+        return carry
+
+    lax.fori_loop(0, steps - per_owner, finish, 0)
+
+
+def project(attended, out_weight):
+    n = lax.axis_size("head")
+    rows, depth = attended.shape
+    columns = out_weight.shape[1] // n
+    chunk = math.gcd(columns, 512)
+    per_owner = columns // chunk
+    in_vmem = pl.BlockSpec(memory_space=pltpu.VMEM)
+    return pl.pallas_call(
+        functools.partial(project_kernel, n, chunk),
+        out_shape=jax.ShapeDtypeStruct((rows, columns), BF16),
+        in_specs=[in_vmem, pl.BlockSpec(memory_space=pl.ANY)],
+        out_specs=in_vmem,
+        scratch_shapes=[
+            pltpu.VMEM((n * per_owner, depth, chunk), BF16),
+            pltpu.VMEM((n + 1, per_owner, rows, chunk), BF16),
+            pltpu.VMEM((rows, chunk), F32),
+            pltpu.SemaphoreType.DMA((n * per_owner,)),
+            pltpu.SemaphoreType.DMA((n + 1, per_owner)),
+            pltpu.SemaphoreType.DMA((n + 1, per_owner)),
+        ],
+        compiler_params=pltpu.CompilerParams(
+            collective_id=2, has_side_effects=True, vmem_limit_bytes=60 * 2**20
+        ),
+    )(attended, out_weight)
 
 
 def per_device(hyena_inputs, short_filter, medium_filter, q_proj, k_proj, out_weight):
-    keys = lax.all_gather(k_proj, "seq", axis=0, tiled=True)
+    key_pieces = earlier_pieces(k_proj)
     hyena_out = filter_block(hyena_inputs, short_filter, medium_filter)
-    values = lax.all_gather(hyena_out, "seq", axis=0, tiled=True)
-    attended = attention(q_proj, keys, values)
-    summed = lax.psum_scatter(
-        lax.dot_general(
-            out_weight, attended, (((0,), (1,)), ((), ())), preferred_element_type=F32
-        ).astype(BF16),
-        "head",
-        scatter_dimension=0,
-        tiled=True,
-    )
-    return (hyena_out, summed.T)
+    attended = attention(q_proj, key_pieces, hyena_out)
+    return (hyena_out, project(attended, out_weight))
 
 
 def solution(mesh):

time: 364 us -> 322 us (0.88)
  waiting for transfers between devices: 256 us -> 52.6 us
  Pallas kernels: 55.9 us -> 249 us
  matrix products: 26 us -> 0 us
  between operations: 13.8 us -> 0.69 us
  starting transfers between devices: 3.95 us -> 10.6 us
    pallas_call x1 -> x2, Pallas kernels: 36.3 us -> 229 us  [the longest x1 166 us: project(): pl.pallas_call(functools.partial(project_kernel, n, chunk), out_shape=jax...]
    reduce_scatter x1 -> x0, waiting for transfers between devices: 156 us -> none  [per_device(): lax.psum_scatter(lax.dot_general(out_weight, attended, (((0,), (1,)), (()...]
    all_gather x2 -> x0, waiting for transfers between devices: 76.2 us -> none  [the longest x1 60.5 us: per_device(): values = lax.all_gather(hyena_out, 'seq', axis=0, tiled=True)]
    ppermute x0 -> x3, waiting for transfers between devices: none -> 45.1 us  [the longest x1 45.1 us: earlier_pieces(): mine.append(lax.ppermute(x, 'seq', pairs))]
    dot_general x1 -> x0, matrix products: 26 us -> none  [per_device(): lax.dot_general(out_weight, attended, (((0,), (1,)), ((), ())), preferred...]
    ppermute x2, waiting for transfers between devices: 23.3 us -> 7.53 us  [passed_along(): return lax.ppermute(x, axis, pairs)]
    ppermute x0 -> x3, starting transfers between devices: none -> 6.3 us  [the longest x2 5.01 us: earlier_pieces(): other.append(lax.ppermute(mine[d], 'seq', pairs))]
  transfers between devices with their start and end apart: 5 -> 5, of which waited for: 4 -> 2; matrix products, arithmetic and copies ran while one was open for 1% -> 1% of each run, Pallas kernels for 5% -> 6%
where the time goes in v2:
time: 322 us; the launch traced here: 321 us
  Pallas kernels  249 us (77%)
  waiting for transfers between devices  52.6 us (16%)
  starting transfers between devices  10.6 us (3%)
  local copies, waits for them, and re-layouts  8.49 us (3%)
    pallas_call x1, Pallas kernels, project(): pl.pallas_call(functools.partial(project_kernel, n, chunk), out_shape=jax...  166 us
    pallas_call x1, Pallas kernels, attention(): pl.pallas_call(functools.partial(attention_kernel, chips, groups), out_sh...  63 us
    ppermute x1, waiting for transfers between devices, earlier_pieces(): mine.append(lax.ppermute(x, 'seq', pairs))  45.1 us
    pallas_call x1, Pallas kernels, filter_block(): pl.pallas_call(filter_kernel, grid=(width // tile,), out_shape=jax.ShapeD...  13.9 us
    ppermute x2, waiting for transfers between devices, passed_along(): return lax.ppermute(x, axis, pairs)  7.53 us
  transfers between devices with their start and end apart: 5, of which 2 were waited for; matrix products, arithmetic and copies ran while one was open for 1% of the time, Pallas kernels for 6%

profile of v2, /device:TPU:14, one launch (start us, length us, event | category | flops | bytes accessed | tf_op | source)
XLA Modules:
  0.0 321.2 jit_solution(14438117584042992762)
XLA Ops:
  0.6 1.3 collective-permute-start.2
  1.9 3.1 collective-permute-start.3
  5.0 45.1 %collective-permute-done.2.refs_1_ = bf16[512,2048]{1,0:T(8,128)(2,1)S(1)} collective-permute-done((bf16[512,2048]{1,0:T(8,128)(2,1)}, bf16[512,2048]{1,0:T(8,128)(2,1)S(1)}, u32[]{:S(2)}, u32[]{:S(2)}) %collective-permute-start.2) | collective-permute-done | bytes 2097184 | tf_op jit(solution)/shard_map/ppermute | solution.py:248
  50.1 0.0 copy-start
  50.1 1.9 collective-permute-start.4
  52.0 2.9 slice.9.x_ref
  54.9 5.6 %shard_map.95 = bf16[128,2048]{1,0:T(8,128)(2,1)} custom-call(bf16[3,144,2048]{2,1,0:T(8,128)(2,1)} %slice.9.x_ref, f32[3,3,2048]{2,1,0:T(4,128)} %short_ref.3), custom_call_target="tpu_custom_call" | custom-call | tf_op jit(solution)/shard_map/pallas_call | solution.py:99
  60.5 0.0 copy-done
  60.5 2.4 collective-permute-start.1
  62.9 0.9 slice.8
  63.8 1.9 collective-permute-start
  65.8 7.5 %collective-permute-done.halo_ref = bf16[3,16,2048]{2,1,0:T(8,128)(2,1)S(1)} collective-permute-done((bf16[3,16,2048]{2,1,0:T(8,128)(2,1)S(1)}, bf16[3,16,2048]{2,1,0:T(8,128)(2,1)S(1)}, u32[]{:S(2)}, u32[]{:S(2)}) %collective-permute-start) | collective-permute-done | bytes 196640 | tf_op jit(solution)/shard_map/ppermute | solution.py:22
  73.3 0.0 copy-start.2
  73.3 0.0 collective-permute-done.1.tail_ref
  73.3 0.7 copy-done.2
  74.0 0.0 copy-start.1
  74.0 0.8 copy-done.1
  74.8 13.9 %shard_map.96.refs_4_ = bf16[512,2048]{1,0:T(8,128)(2,1)} custom-call(bf16[3,512,2048]{2,1,0:T(8,128)(2,1)} %bitcast.3, bf16[3,16,2048]{2,1,0:T(8,128)(2,1)} %copy-done.2, bf16[128,2048]{1,0:T(8,128)(2,1)} %copy-done.1, f32[3,3,2048]{2,1,0:T(4,128)} %short_ref.3, f32[128,2048]{1,0:T(8,128)} %medium_ref.1, bf16[2,256,256]{2,1,0:T(8,128)(2,1)} %constant.4.clone.fwd_ref, ...), custom_call_target="tpu_custom_call" | custom-call | tf_op jit(solution)/shard_map/pallas_call | solution.py:108
  88.7 0.0 collective-permute-done.3.refs_2_
  88.7 0.0 collective-permute-done.4.refs_3_
  88.7 63.0 %shard_map.97.att_ref = bf16[512,2048]{1,0:T(8,128)(2,1)} custom-call(bf16[512,2048]{1,0:T(8,128)(2,1)} %q_ref.1, bf16[512,2048]{1,0:T(8,128)(2,1)} %refs_0_.1, bf16[512,2048]{1,0:T(8,128)(2,1)} %copy-done, bf16[512,2048]{1,0:T(8,128)(2,1)} %collective-permute-done.3.refs_2_, bf16[512,2048]{1,0:T(8,128)(2,1)} %collective-permute-done.4.refs_3_, ...), custom_call_target="tpu_custom_call" | custom-call | tf_op jit(solution)/shard_map/pallas_call | solution.py:262
  151.7 166.3 %shard_map.98 = bf16[512,2048]{1,0:T(8,128)(2,1)} custom-call(bf16[512,2048]{1,0:T(8,128)(2,1)} %shard_map.97.att_ref, bf16[2048,8192]{1,0:T(8,128)(2,1)} %w_ref.1), custom_call_target="tpu_custom_call" | custom-call | tf_op jit(solution)/shard_map/pallas_call | solution.py:400
  318.0 3.2 copy.11
Async XLA Ops:
  0.6 49.5 %collective-permute-start.2 = (bf16[512,2048]{1,0:T(8,128)(2,1)}, bf16[512,2048]{1,0:T(8,128)(2,1)S(1)}, u32[]{:S(2)}, u32[]{:S(2)}) collective-permute-start(bf16[512,2048]{1,0:T(8,128)(2,1)} %refs_0_.1), channel_id=1, source_target_pairs={{0,16},{8,24},{1,17},{9,25},{2,18},{10,26},{3,19},{11,27},{4,20},{... | collective-permute-start | bytes 6291464 | tf_op jit(solution)/shard_map/ppermute | solution.py:248
  1.9 86.8 %collective-permute-start.3 = (bf16[512,2048]{1,0:T(8,128)(2,1)}, bf16[512,2048]{1,0:T(8,128)(2,1)}, u32[]{:S(2)}, u32[]{:S(2)}) collective-permute-start(bf16[512,2048]{1,0:T(8,128)(2,1)} %refs_0_.1), channel_id=1, source_target_pairs={{0,8},{16,24},{1,9},{17,25},{2,10},{18,26},{3,11},{19,27},{4,12},{... | collective-permute-start | bytes 6291464 | tf_op jit(solution)/shard_map/ppermute | solution.py:253
  50.1 10.4 %copy-start = (bf16[512,2048]{1,0:T(8,128)(2,1)}, bf16[512,2048]{1,0:T(8,128)(2,1)S(1)}, u32[]{:S(2)}) copy-start(bf16[512,2048]{1,0:T(8,128)(2,1)S(1)} %collective-permute-done.2.refs_1_) | copy-start | bytes 6291460
  50.1 38.6 %collective-permute-start.4 = (bf16[512,2048]{1,0:T(8,128)(2,1)S(1)}, bf16[512,2048]{1,0:T(8,128)(2,1)}, u32[]{:S(2)}, u32[]{:S(2)}) collective-permute-start(bf16[512,2048]{1,0:T(8,128)(2,1)S(1)} %collective-permute-done.2.refs_1_), channel_id=1, source_target_pairs={{16,24},{24,16},{17,25},{25,17},{18,26},{26,18},{19,27},{27,19},{2... | collective-permute-start | bytes 6291464 | tf_op jit(solution)/shard_map/ppermute | solution.py:253
  60.5 12.8 %collective-permute-start.1 = (bf16[128,2048]{1,0:T(8,128)(2,1)}, bf16[128,2048]{1,0:T(8,128)(2,1)S(1)}, u32[]{:S(2)}, u32[]{:S(2)}) collective-permute-start(bf16[128,2048]{1,0:T(8,128)(2,1)} %shard_map.95), channel_id=1, source_target_pairs={{0,8},{8,16},{16,24},{1,9},{9,17},{17,25},{2,10},{10,18},{18,26},{... | collective-permute-start | bytes 1572872 | tf_op jit(solution)/shard_map/ppermute | solution.py:22
  63.8 9.5 %collective-permute-start = (bf16[3,16,2048]{2,1,0:T(8,128)(2,1)S(1)}, bf16[3,16,2048]{2,1,0:T(8,128)(2,1)S(1)}, u32[]{:S(2)}, u32[]{:S(2)}) collective-permute-start(bf16[3,16,2048]{2,1,0:T(8,128)(2,1)S(1)} %slice.8), channel_id=1, source_target_pairs={{0,8},{8,16},{16,24},{1,9},{9,17},{17,25},{2,10},{10,18},{18,26},{... | collective-permute-start | bytes 589832 | tf_op jit(solution)/shard_map/ppermute | solution.py:22
  73.3 0.7 copy-start.2
  74.0 0.8 copy-start.1

commit v3 on v2

--- a/solution.py
+++ b/solution.py
@@ -55,7 +55,8 @@
 
 
 def tail_kernel(x_ref, short_ref, out_ref):
-    parts = [short_filtered(x_ref[i].astype(F32), short_ref, i) for i in (1, 2)]
+    start = x_ref.shape[1] - out_ref.shape[0] - MARGIN
+    parts = [short_filtered(x_ref[i, start:].astype(F32), short_ref, i) for i in (1, 2)]
     out_ref[...] = (parts[0] * parts[1]).astype(BF16)
 
 
@@ -93,16 +94,18 @@
     taps = medium_filter.shape[0]
     tile = min(256, width)
     halo = passed_along(x[:, rows - MARGIN :], "seq", 1)
-    tail_rows = x[:, rows - taps - MARGIN :]
     by_col = lambda *lead: pl.BlockSpec((*lead, tile), lambda c: (0,) * len(lead) + (c,))
     whole = lambda a: pl.BlockSpec(a.shape, lambda c: (0,) * a.ndim)
     tail = pl.pallas_call(
         tail_kernel,
         grid=(width // tile,),
         out_shape=jax.ShapeDtypeStruct((taps, width), BF16),
-        in_specs=[by_col(3, taps + MARGIN), by_col(3, short_filter.shape[1])],
+        in_specs=[
+            pl.BlockSpec((3, rows // 2, tile), lambda c: (0, 1, c)),
+            by_col(3, short_filter.shape[1]),
+        ],
         out_specs=by_col(taps),
-    )(tail_rows, short_filter)
+    )(x, short_filter)
     tail = passed_along(tail, "seq", 1)
     forward, inverse = transform_tables(taps)
     return pl.pallas_call(
@@ -124,9 +127,11 @@
 
 
 def attention_kernel(chips, groups, q_ref, *refs):
-    pieces = 2 * chips
-    key_refs, own_ref = refs[:pieces], refs[pieces]
-    out_ref, got, acc, top, total, send_sem, recv_sem = refs[pieces + 1 :]
+    key_refs, own_ref = refs[:chips], refs[chips]
+    (
+        out_ref, got, got_keys, acc, top, total,
+        send_sem, recv_sem, key_send_sem, key_recv_sem,
+    ) = refs[chips + 1 :]
     rows = q_ref.shape[0]
     group_width = q_ref.shape[1] // groups
     me = lax.axis_index("seq")
@@ -164,10 +169,24 @@
             device_id_type=MESH,
         )
 
+    def beside_keys(d, g):
+        span = pl.ds(pl.multiple_of(g * group_width, HEAD_SIZE), group_width)
+        return pltpu.make_async_remote_copy(
+            src_ref=key_refs[d].at[:, span],
+            dst_ref=got_keys.at[d, :, span],
+            send_sem=key_send_sem.at[d, g],
+            recv_sem=key_recv_sem.at[d, g],
+            device_id={"seq": partner},
+            device_id_type=MESH,
+        )
+
     def send_group(g, carry):
         for d in range(1, chips):
             pl.when(chip + d < chips)(lambda d=d: across(d, g).start())
+        pl.when(core == 0)(lambda: beside_keys(0, g).start())
         pl.when(core == 0)(lambda: beside(0, g).start())
+        for d in range(1, chips):
+            pl.when(chip >= d)(lambda d=d: beside_keys(d, g).start())
         return carry
 
     lax.fori_loop(0, groups, send_group, 0)
@@ -203,9 +222,17 @@
                 across(d, g).wait_recv()
                 beside(d, g).start()
 
-        pl.when(core == 1)(lambda: beside(0, g).wait_recv())
+        @pl.when(core == 1)
+        def _():
+            beside_keys(0, g).wait_recv()
+            beside(0, g).wait_recv()
+
         for d in range(1, chips):
-            pl.when(chip >= d)(lambda d=d: beside(d, g).wait_recv())
+
+            @pl.when(chip >= d)
+            def _():
+                beside_keys(d, g).wait_recv()
+                beside(d, g).wait_recv()
 
         def one_head(h, carry):
             cols = pl.ds(pl.multiple_of(g * group_width + h * HEAD_SIZE, HEAD_SIZE), HEAD_SIZE)
@@ -214,14 +241,14 @@
 
             @pl.when(core == 1)
             def _():
-                visit((key_refs[chips][:, cols], queries), got[chips - 1, :, cols], False)
+                visit((got_keys[0, :, cols], queries), got[chips - 1, :, cols], False)
 
             for d in range(1, chips):
 
                 @pl.when(chip >= d)
                 def _():
                     visit((key_refs[d][:, cols], queries), got[d - 1, :, cols], False)
-                    visit((key_refs[chips + d][:, cols], queries), got[chips - 1 + d, :, cols], False)
+                    visit((got_keys[d, :, cols], queries), got[chips - 1 + d, :, cols], False)
 
             out_ref[:, cols] = (acc[...] / total[...]).T.astype(BF16)
             return carry
@@ -234,7 +261,9 @@
         for d in range(1, chips):
             pl.when(chip + d < chips)(lambda d=d: across(d, g).wait_send())
             pl.when(chip >= d)(lambda d=d: beside(d, g).wait_send())
+            pl.when(chip >= d)(lambda d=d: beside_keys(d, g).wait_send())
         pl.when(core == 0)(lambda: beside(0, g).wait_send())
+        pl.when(core == 0)(lambda: beside_keys(0, g).wait_send())
         return carry
 
     lax.fori_loop(0, groups, finish, 0)
@@ -242,35 +271,33 @@
 
 def earlier_pieces(x):
     chips = lax.axis_size("seq") // 2
-    mine, other = [x], []
+    mine = [x]
     for d in range(1, chips):
         pairs = [(2 * i + k, 2 * (i + d) + k) for i in range(chips - d) for k in range(2)]
         mine.append(lax.ppermute(x, "seq", pairs))
-    for d in range(chips):
-        pairs = [(2 * i, 2 * i + 1) for i in range(d, chips)]
-        if d > 0:
-            pairs += [(2 * i + 1, 2 * i) for i in range(d, chips)]
-        other.append(lax.ppermute(mine[d], "seq", pairs))
-    return mine + other
+    return mine
 
 
 def attention(q, key_pieces, values):
     rows, width = q.shape
-    chips = len(key_pieces) // 2
+    chips = len(key_pieces)
     groups = math.gcd(width // HEAD_SIZE, 8)
     in_vmem = pl.BlockSpec(memory_space=pltpu.VMEM)
     return pl.pallas_call(
         functools.partial(attention_kernel, chips, groups),
         out_shape=jax.ShapeDtypeStruct((rows, width), BF16),
-        in_specs=[in_vmem] * (2 * chips + 2),
+        in_specs=[in_vmem] * (chips + 2),
         out_specs=in_vmem,
         scratch_shapes=[
             pltpu.VMEM((2 * chips - 1, rows, width), BF16),
+            pltpu.VMEM((chips, rows, width), BF16),
             pltpu.VMEM((HEAD_SIZE, rows), F32),
             pltpu.VMEM((1, rows), F32),
             pltpu.VMEM((1, rows), F32),
             pltpu.SemaphoreType.DMA((2 * chips - 1, groups)),
             pltpu.SemaphoreType.DMA((2 * chips - 1, groups)),
+            pltpu.SemaphoreType.DMA((chips, groups)),
+            pltpu.SemaphoreType.DMA((chips, groups)),
         ],
         compiler_params=pltpu.CompilerParams(
             collective_id=1, has_side_effects=True, vmem_limit_bytes=56 * 2**20

time: 322 us -> 306 us (0.950)
  waiting for transfers between devices: 52.6 us -> 45.2 us
  starting transfers between devices: 10.6 us -> 5.12 us
    ppermute x1, waiting for transfers between devices: 45.1 us -> 0.01 us  [earlier_pieces(): mine.append(lax.ppermute(x, 'seq', pairs))]
    ppermute x2, waiting for transfers between devices: 7.53 us -> 45.2 us  [passed_along(): return lax.ppermute(x, axis, pairs)]
    ppermute x2 -> x0, starting transfers between devices: 5.01 us -> none  [earlier_pieces(): other.append(lax.ppermute(mine[d], 'seq', pairs))]
  transfers between devices with their start and end apart: 5 -> 3, of which waited for: 2 -> 1; matrix products, arithmetic and copies ran while one was open for 1% -> 0% of each run, Pallas kernels for 6% -> 6%
where the time goes in v3:
time: 306 us
  Pallas kernels  248 us (81%)
  waiting for transfers between devices  45.2 us (15%)
  local copies, waits for them, and re-layouts  6.88 us (2%)
  starting transfers between devices  5.12 us (2%)
    pallas_call x1, Pallas kernels, project(): pl.pallas_call(functools.partial(project_kernel, n, chunk), out_shape=jax...  166 us
    pallas_call x1, Pallas kernels, attention(): pl.pallas_call(functools.partial(attention_kernel, chips, groups), out_sh...  62.1 us
    ppermute x2, waiting for transfers between devices, passed_along(): return lax.ppermute(x, axis, pairs)  45.2 us
    pallas_call x1, Pallas kernels, filter_block(): pl.pallas_call(filter_kernel, grid=(width // tile,), out_shape=jax.ShapeD...  13.9 us
  transfers between devices with their start and end apart: 3, of which 1 were waited for; matrix products, arithmetic and copies ran while one was open for 0% of the time, Pallas kernels for 6%

profile of v3, /device:TPU:14, one launch (start us, length us, event | category | flops | bytes accessed | tf_op | source)
XLA Modules:
  0.0 305.6 jit_solution(3831696120471222565)
XLA Ops:
  0.6 1.3 collective-permute-start.2
  1.9 5.9 %shard_map.95 = bf16[128,2048]{1,0:T(8,128)(2,1)} custom-call(bf16[3,512,2048]{2,1,0:T(8,128)(2,1)} %bitcast.1, f32[3,3,2048]{2,1,0:T(4,128)} %short_ref.3), custom_call_target="tpu_custom_call" | custom-call | tf_op jit(solution)/shard_map/pallas_call | solution.py:99
  7.8 1.9 collective-permute-start.1
  9.7 0.9 slice.4
  10.7 1.9 collective-permute-start
  12.6 45.2 %collective-permute-done.halo_ref = bf16[3,16,2048]{2,1,0:T(8,128)(2,1)S(1)} collective-permute-done((bf16[3,16,2048]{2,1,0:T(8,128)(2,1)S(1)}, bf16[3,16,2048]{2,1,0:T(8,128)(2,1)S(1)}, u32[]{:S(2)}, u32[]{:S(2)}) %collective-permute-start) | collective-permute-done | bytes 196640 | tf_op jit(solution)/shard_map/ppermute | solution.py:22
  57.8 0.0 copy-start.2
  57.8 0.0 collective-permute-done.1.tail_ref
  57.8 0.7 copy-done.2
  58.5 0.0 copy-start.1
  58.5 0.8 copy-done.1
  59.3 13.9 %shard_map.96.refs_2_ = bf16[512,2048]{1,0:T(8,128)(2,1)} custom-call(bf16[3,512,2048]{2,1,0:T(8,128)(2,1)} %bitcast.3, bf16[3,16,2048]{2,1,0:T(8,128)(2,1)} %copy-done.2, bf16[128,2048]{1,0:T(8,128)(2,1)} %copy-done.1, f32[3,3,2048]{2,1,0:T(4,128)} %short_ref.3, f32[128,2048]{1,0:T(8,128)} %medium_ref.1, bf16[2,256,256]{2,1,0:T(8,128)(2,1)} %constant.4.clone.fwd_ref, ...), custom_call_target="tpu_custom_call" | custom-call | tf_op jit(solution)/shard_map/pallas_call | solution.py:111
  73.2 0.0 collective-permute-done.2.refs_1_
  73.2 0.0 copy-start
  73.2 1.3 copy-done
  74.6 62.1 %shard_map.97.att_ref = bf16[512,2048]{1,0:T(8,128)(2,1)} custom-call(bf16[512,2048]{1,0:T(8,128)(2,1)} %q_ref.1, bf16[512,2048]{1,0:T(8,128)(2,1)} %refs_0_.1, bf16[512,2048]{1,0:T(8,128)(2,1)} %copy-done, bf16[512,2048]{1,0:T(8,128)(2,1)} %shard_map.96.refs_2_), custom_call_target="tpu_custom_call" | custom-call | tf_op jit(solution)/shard_map/pallas_call | solution.py:286
  136.7 165.8 %shard_map.98 = bf16[512,2048]{1,0:T(8,128)(2,1)} custom-call(bf16[512,2048]{1,0:T(8,128)(2,1)} %shard_map.97.att_ref, bf16[2048,8192]{1,0:T(8,128)(2,1)} %w_ref.1), custom_call_target="tpu_custom_call" | custom-call | tf_op jit(solution)/shard_map/pallas_call | solution.py:427
  302.5 3.2 %copy.11 = bf16[512,2048]{1,0:T(8,128)(2,1)} copy(bf16[512,2048]{1,0:T(8,128)(2,1)} %shard_map.98) | data formatting | bytes 4194304
Async XLA Ops:
  0.6 72.6 %collective-permute-start.2 = (bf16[512,2048]{1,0:T(8,128)(2,1)}, bf16[512,2048]{1,0:T(8,128)(2,1)S(1)}, u32[]{:S(2)}, u32[]{:S(2)}) collective-permute-start(bf16[512,2048]{1,0:T(8,128)(2,1)} %refs_0_.1), channel_id=1, source_target_pairs={{0,16},{8,24},{1,17},{9,25},{2,18},{10,26},{3,19},{11,27},{4,20},{... | collective-permute-start | bytes 6291464 | tf_op jit(solution)/shard_map/ppermute | solution.py:277
  7.8 50.0 %collective-permute-start.1 = (bf16[128,2048]{1,0:T(8,128)(2,1)}, bf16[128,2048]{1,0:T(8,128)(2,1)S(1)}, u32[]{:S(2)}, u32[]{:S(2)}) collective-permute-start(bf16[128,2048]{1,0:T(8,128)(2,1)} %shard_map.95), channel_id=1, source_target_pairs={{0,8},{8,16},{16,24},{1,9},{9,17},{17,25},{2,10},{10,18},{18,26},{... | collective-permute-start | bytes 1572872 | tf_op jit(solution)/shard_map/ppermute | solution.py:22
  10.7 47.2 %collective-permute-start = (bf16[3,16,2048]{2,1,0:T(8,128)(2,1)S(1)}, bf16[3,16,2048]{2,1,0:T(8,128)(2,1)S(1)}, u32[]{:S(2)}, u32[]{:S(2)}) collective-permute-start(bf16[3,16,2048]{2,1,0:T(8,128)(2,1)S(1)} %slice.4), channel_id=1, source_target_pairs={{0,8},{8,16},{16,24},{1,9},{9,17},{17,25},{2,10},{10,18},{18,26},{... | collective-permute-start | bytes 589832 | tf_op jit(solution)/shard_map/ppermute | solution.py:22
  57.8 0.7 copy-start.2
  58.5 0.8 copy-start.1
  73.2 1.3 copy-start

commit v4 on v3

--- a/solution.py
+++ b/solution.py
@@ -88,7 +88,7 @@
         out_ref[span, :] = (filtered[0][span] * medium).astype(BF16)
 
 
-def filter_block(hyena_inputs, short_filter, medium_filter):
+def filter_block(hyena_inputs, short_filter, medium_filter, k_proj):
     x = jnp.transpose(hyena_inputs, (1, 0, 2))
     _, rows, width = x.shape
     taps = medium_filter.shape[0]
@@ -107,8 +107,10 @@
         out_specs=by_col(taps),
     )(x, short_filter)
     tail = passed_along(tail, "seq", 1)
+    tail, halo, k_proj = lax.optimization_barrier((tail, halo, k_proj))
+    key_pieces = earlier_pieces(k_proj)
     forward, inverse = transform_tables(taps)
-    return pl.pallas_call(
+    hyena_out = pl.pallas_call(
         filter_kernel,
         grid=(width // tile,),
         out_shape=jax.ShapeDtypeStruct((rows, width), BF16),
@@ -124,6 +126,7 @@
         out_specs=by_col(rows),
         compiler_params=pltpu.CompilerParams(vmem_limit_bytes=56 * 2**20),
     )(x, halo, tail, short_filter, medium_filter, jnp.asarray(forward), jnp.asarray(inverse))
+    return hyena_out, key_pieces
 
 
 def attention_kernel(chips, groups, q_ref, *refs):
@@ -444,8 +447,7 @@
 
 
 def per_device(hyena_inputs, short_filter, medium_filter, q_proj, k_proj, out_weight):
-    key_pieces = earlier_pieces(k_proj)
-    hyena_out = filter_block(hyena_inputs, short_filter, medium_filter)
+    hyena_out, key_pieces = filter_block(hyena_inputs, short_filter, medium_filter, k_proj)
     attended = attention(q_proj, key_pieces, hyena_out)
     return (hyena_out, project(attended, out_weight))
 

time: 306 us -> 299 us (0.977)
  waiting for transfers between devices: 45.2 us -> 39.5 us
    ppermute x2, waiting for transfers between devices: 45.2 us -> 8.01 us  [passed_along(): return lax.ppermute(x, axis, pairs)]
    ppermute x1, waiting for transfers between devices: 0.01 us -> 31.4 us  [earlier_pieces(): mine.append(lax.ppermute(x, 'seq', pairs))]
  transfers between devices with their start and end apart: 3 -> 3, of which waited for: 1 -> 2; matrix products, arithmetic and copies ran while one was open for 0% -> 0% of each run, Pallas kernels for 6% -> 5%
where the time goes in v4:
time: 299 us
  Pallas kernels  248 us (83%)
  waiting for transfers between devices  39.5 us (13%)
  local copies, waits for them, and re-layouts  5.44 us (2%)
  starting transfers between devices  5.12 us (2%)
    pallas_call x1, Pallas kernels, project(): pl.pallas_call(functools.partial(project_kernel, n, chunk), out_shape=jax...  166 us
    pallas_call x1, Pallas kernels, attention(): pl.pallas_call(functools.partial(attention_kernel, chips, groups), out_sh...  62.1 us
    ppermute x1, waiting for transfers between devices, earlier_pieces(): mine.append(lax.ppermute(x, 'seq', pairs))  31.4 us
    pallas_call x1, Pallas kernels, filter_block(): pl.pallas_call(filter_kernel, grid=(width // tile,), out_shape=jax.ShapeD...  14 us
    ppermute x2, waiting for transfers between devices, passed_along(): return lax.ppermute(x, axis, pairs)  8.01 us
    pallas_call x1, Pallas kernels, filter_block(): pl.pallas_call(tail_kernel, grid=(width // tile,), out_shape=jax.ShapeDty...  6.02 us
  transfers between devices with their start and end apart: 3, of which 2 were waited for; matrix products, arithmetic and copies ran while one was open for 0% of the time, Pallas kernels for 5%

profile of v4, /device:TPU:14, one launch (start us, length us, event | category | flops | bytes accessed | tf_op | source)
XLA Modules:
  0.0 298.7 jit_solution(85854063123987982)
XLA Ops:
  0.6 0.0 copy-start
  0.6 6.0 %shard_map.95 = bf16[128,2048]{1,0:T(8,128)(2,1)} custom-call(bf16[3,512,2048]{2,1,0:T(8,128)(2,1)} %bitcast.1, f32[3,3,2048]{2,1,0:T(4,128)} %short_ref.3), custom_call_target="tpu_custom_call" | custom-call | tf_op jit(solution)/shard_map/pallas_call | solution.py:99
  6.7 1.9 collective-permute-start
  8.6 0.9 slice.4
  9.5 1.9 collective-permute-start.1
  11.5 8.0 %collective-permute-done.1.halo_ref = bf16[3,16,2048]{2,1,0:T(8,128)(2,1)S(1)} collective-permute-done((bf16[3,16,2048]{2,1,0:T(8,128)(2,1)S(1)}, bf16[3,16,2048]{2,1,0:T(8,128)(2,1)S(1)}, u32[]{:S(2)}, u32[]{:S(2)}) %collective-permute-start.1) | collective-permute-done | bytes 196640 | tf_op jit(solution)/shard_map/ppermute | solution.py:22
  19.5 0.0 copy-start.3
  19.5 0.0 collective-permute-done.tail_ref
  19.5 0.0 copy-done
  19.5 0.0 copy-start.2
  19.5 1.3 collective-permute-start.2
  20.8 0.0 copy-done.3
  20.8 0.0 copy-done.2
  20.8 14.0 %shard_map.96.refs_2_ = bf16[512,2048]{1,0:T(8,128)(2,1)} custom-call(bf16[3,512,2048]{2,1,0:T(8,128)(2,1)} %bitcast.3, bf16[3,16,2048]{2,1,0:T(8,128)(2,1)} %copy-done.3, bf16[128,2048]{1,0:T(8,128)(2,1)} %copy-done.2, f32[3,3,2048]{2,1,0:T(4,128)} %short_ref.3, f32[128,2048]{1,0:T(8,128)} %medium_ref.1, bf16[2,256,256]{2,1,0:T(8,128)(2,1)} %constant.4.clone.fwd_ref, ...), custom_call_target="tpu_custom_call" | custom-call | tf_op jit(solution)/shard_map/pallas_call | solution.py:113
  34.8 31.4 %collective-permute-done.2.refs_1_ = bf16[512,2048]{1,0:T(8,128)(2,1)S(1)} collective-permute-done((bf16[512,2048]{1,0:T(8,128)(2,1)S(1)}, bf16[512,2048]{1,0:T(8,128)(2,1)S(1)}, u32[]{:S(2)}, u32[]{:S(2)}) %collective-permute-start.2) | collective-permute-done | bytes 2097184 | tf_op jit(solution)/shard_map/ppermute | solution.py:280
  66.2 0.0 copy-start.1
  66.2 1.3 copy-done.1
  67.5 62.1 %shard_map.97.att_ref = bf16[512,2048]{1,0:T(8,128)(2,1)} custom-call(bf16[512,2048]{1,0:T(8,128)(2,1)} %q_ref.1, bf16[512,2048]{1,0:T(8,128)(2,1)} %refs_0_, bf16[512,2048]{1,0:T(8,128)(2,1)} %copy-done.1, bf16[512,2048]{1,0:T(8,128)(2,1)} %shard_map.96.refs_2_), custom_call_target="tpu_custom_call" | custom-call | tf_op jit(solution)/shard_map/pallas_call | solution.py:289
  129.7 165.9 %shard_map.98 = bf16[512,2048]{1,0:T(8,128)(2,1)} custom-call(bf16[512,2048]{1,0:T(8,128)(2,1)} %shard_map.97.att_ref, bf16[2048,8192]{1,0:T(8,128)(2,1)} %w_ref.1), custom_call_target="tpu_custom_call" | custom-call | tf_op jit(solution)/shard_map/pallas_call | solution.py:430
  295.6 3.2 %copy.11 = bf16[512,2048]{1,0:T(8,128)(2,1)} copy(bf16[512,2048]{1,0:T(8,128)(2,1)} %shard_map.98) | data formatting | bytes 4194304
Async XLA Ops:
  0.6 18.8 %copy-start = (bf16[512,2048]{1,0:T(8,128)(2,1)S(1)}, bf16[512,2048]{1,0:T(8,128)(2,1)}, u32[]{:S(2)}) copy-start(bf16[512,2048]{1,0:T(8,128)(2,1)} %refs_0_) | copy-start | bytes 6291460
  6.7 12.8 %collective-permute-start = (bf16[128,2048]{1,0:T(8,128)(2,1)}, bf16[128,2048]{1,0:T(8,128)(2,1)S(1)}, u32[]{:S(2)}, u32[]{:S(2)}) collective-permute-start(bf16[128,2048]{1,0:T(8,128)(2,1)} %shard_map.95), channel_id=1, source_target_pairs={{0,8},{8,16},{16,24},{1,9},{9,17},{17,25},{2,10},{10,18},{18,26},{... | collective-permute-start | bytes 1572872 | tf_op jit(solution)/shard_map/ppermute | solution.py:22
  9.5 9.9 %collective-permute-start.1 = (bf16[3,16,2048]{2,1,0:T(8,128)(2,1)S(1)}, bf16[3,16,2048]{2,1,0:T(8,128)(2,1)S(1)}, u32[]{:S(2)}, u32[]{:S(2)}) collective-permute-start(bf16[3,16,2048]{2,1,0:T(8,128)(2,1)S(1)} %slice.4), channel_id=1, source_target_pairs={{0,8},{8,16},{16,24},{1,9},{9,17},{17,25},{2,10},{10,18},{18,26},{... | collective-permute-start | bytes 589832 | tf_op jit(solution)/shard_map/ppermute | solution.py:22
  19.5 1.3 copy-start.3
  19.5 1.3 copy-start.2
  19.5 46.7 %collective-permute-start.2 = (bf16[512,2048]{1,0:T(8,128)(2,1)S(1)}, bf16[512,2048]{1,0:T(8,128)(2,1)S(1)}, u32[]{:S(2)}, u32[]{:S(2)}) collective-permute-start(bf16[512,2048]{1,0:T(8,128)(2,1)S(1)} %copy-done), channel_id=1, source_target_pairs={{0,16},{8,24},{1,17},{9,25},{2,18},{10,26},{3,19},{11,27},{4,20},{... | collective-permute-start | bytes 6291464 | tf_op jit(solution)/shard_map/ppermute | solution.py:280
  66.2 1.3 copy-start.1
